TPU v7x, 128 devices: a whole 4x4x4 slice. The times are simulated.
128 devices in a mesh: rows: 16 (over y_hi, x, core), cols: 8 (over z, y_lo).
Axes of the slice: x: 4, y: 4 (y_hi: 2, y_lo: 2; y = y_hi * 2 + y_lo), z: 4, core: 2. Of those that a mesh axis runs over, the one named last changes fastest.
Arguments:
- inputs: bfloat16 [112, 224, 512], P('rows', 'cols'), may hold values from -16 to 16
- cotangent: bfloat16 [112, 224, 512], P('rows', 'cols'), may hold values from -4 to 4
- conv_gain: float32 [512], replicated, may hold values from 0.25 to 1.75
- expand_weight: bfloat16 [512, 2048], replicated, may hold values from -0.25 to 0.25
- depth_weight: float32 [9, 2048], replicated, may hold values from -2 to 2
- project_weight: bfloat16 [2048, 512], replicated, may hold values from -0.125 to 0.125
- block_gain: float32 [512], replicated, may hold values from 0.25 to 1.75
- block_qkv: bfloat16 [512, 1536], replicated, may hold values from -0.25 to 0.25
- block_out: bfloat16 [512, 512], replicated, may hold values from -0.25 to 0.25
- block_bias: float32 [16, 49, 49], replicated, may hold values from -4 to 320
- grid_gain: float32 [512], replicated, may hold values from 0.25 to 1.75
- grid_qkv: bfloat16 [512, 1536], replicated, may hold values from -0.25 to 0.25
- grid_out: bfloat16 [512, 512], replicated, may hold values from -0.25 to 0.25
- grid_bias: float32 [16, 49, 49], replicated, may hold values from -4 to 320
Outputs:
- output: bfloat16 [112, 224, 512], P('rows', 'cols')
- grad_inputs: bfloat16 [112, 224, 512], P('rows', 'cols')
All inputs are finite; a program needn't handle non-finite values.
Results may differ from a plain program's by a relative error of at most 0.03.
Values may be sent and summed in bfloat16 or wider, within the bound.
A program may use at most 128 MiB of HBM per device.

v0:
```python
import jax
import jax.numpy as jnp
from jax import lax
from jax.sharding import PartitionSpec as P

HEADS = 16
HEAD_DIM = 32
WIN = 7


EPSILON = 1e-05


def with_halo(block, sides, width):
    for axis, dim in sides:
        count = lax.axis_size(axis)
        forward = [(i, i + 1) for i in range(count - 1)]
        backward = [(target, source) for source, target in forward]
        low = lax.ppermute(
            lax.slice_in_dim(block, block.shape[dim] - width, None, axis=dim), axis, forward
        )
        high = lax.ppermute(lax.slice_in_dim(block, 0, width, axis=dim), axis, backward)
        block = jnp.concatenate([low, block, high], axis=dim)
    return block


def layer_norm(values, norm_gain):
    floats = values.astype(jnp.float32)
    center = jnp.mean(floats, axis=-1, keepdims=True)
    spread = jnp.mean(jnp.square(floats - center), axis=-1, keepdims=True)
    return (floats - center) * lax.rsqrt(spread + EPSILON) * norm_gain


def attend(windows, norm_gain, qkv_weight, out_weight, bias_table):
    window_count, length, channels = windows.shape
    flattened = windows.reshape(window_count * length, channels)
    normed = layer_norm(flattened, norm_gain).astype(jnp.bfloat16)
    packed = jnp.dot(normed, qkv_weight, preferred_element_type=jnp.float32).astype(jnp.bfloat16)
    packed = packed.reshape(window_count, length, 3, HEADS, HEAD_DIM)
    queries = packed[:, :, 0]
    attn_keys = packed[:, :, 1]
    value_rows = packed[:, :, 2]
    scores = jnp.einsum("wqhd,wkhd->whqk", queries, attn_keys, preferred_element_type=jnp.float32)
    scores = scores * HEAD_DIM ** (-0.5) + bias_table
    weights = jax.nn.softmax(scores, axis=-1).astype(jnp.bfloat16)
    attended = jnp.einsum(
        "whqk,wkhd->wqhd", weights, value_rows, preferred_element_type=jnp.float32
    )
    attended = attended.astype(jnp.bfloat16).reshape(window_count * length, channels)
    summed = flattened.astype(jnp.float32) + jnp.dot(
        attended, out_weight, preferred_element_type=jnp.float32
    )
    return summed.astype(jnp.bfloat16).reshape(window_count, length, channels)


def depthwise(padded, depth_weight, rows_here, cols_here):
    summed = jnp.zeros((rows_here, cols_here, padded.shape[-1]), jnp.float32)
    for row_off in range(3):
        for col_off in range(3):
            summed = (
                summed
                + padded[row_off : row_off + rows_here, col_off : col_off + cols_here]
                * depth_weight[3 * row_off + col_off]
            )
    return summed


def depthwise_back(grad_padded, depth_weight, rows_here, cols_here):
    summed = jnp.zeros((rows_here, cols_here, grad_padded.shape[-1]), jnp.float32)
    for row_off in range(3):
        for col_off in range(3):
            shifted = grad_padded[
                2 - row_off : 2 - row_off + rows_here, 2 - col_off : 2 - col_off + cols_here
            ]
            summed = summed + shifted * depth_weight[3 * row_off + col_off]
    return summed


def to_blocks(spatial):
    rows_here, cols_here, channels = spatial.shape
    windows = spatial.reshape(rows_here // WIN, WIN, cols_here // WIN, WIN, channels).transpose(
        0, 2, 1, 3, 4
    )
    return windows.reshape(-1, WIN * WIN, channels)


def from_blocks(windows, rows_here, cols_here):
    channels = windows.shape[-1]
    spatial = windows.reshape(rows_here // WIN, cols_here // WIN, WIN, WIN, channels).transpose(
        0, 2, 1, 3, 4
    )
    return spatial.reshape(rows_here, cols_here, channels)


def pick_groups(blocks, group_ids, usable):
    picked = jnp.take(blocks, jnp.minimum(group_ids, blocks.shape[0] - 1), axis=0)
    shaped = usable.reshape((-1,) + (1,) * (blocks.ndim - 1))
    return jnp.where(shaped, picked, jnp.zeros_like(picked))


def send_slots(blocks, device_count, sender):
    capacity = (WIN + device_count - 1) // device_count
    slot_ids = jnp.arange(capacity * device_count, dtype=jnp.int32)
    target = slot_ids % device_count
    group_ids = (target - WIN * sender) % device_count + slot_ids // device_count * device_count
    return pick_groups(blocks, group_ids, group_ids < WIN)


def receive_slots(received, device_count, target):
    grid_pos = jnp.arange(WIN, dtype=jnp.int32) * device_count + target
    source = grid_pos // WIN
    column = (grid_pos - WIN * source) // device_count
    return jnp.take(received, column * device_count + source, axis=0)


def return_slots(blocks, device_count, target):
    capacity = (WIN + device_count - 1) // device_count
    slot_ids = jnp.arange(capacity * device_count, dtype=jnp.int32)
    source = slot_ids % device_count
    group_ids = (target - WIN * source) % device_count + slot_ids // device_count * device_count
    position = (WIN * source + group_ids) // device_count
    return pick_groups(blocks, position, group_ids < WIN)


def restore_slots(received, device_count, sender):
    local_ids = jnp.arange(WIN, dtype=jnp.int32)
    column = local_ids // device_count
    source = (WIN * sender + local_ids) % device_count
    return jnp.take(received, column * device_count + source, axis=0)


def to_grid(spatial):
    rows_here, cols_here, channels = spatial.shape
    depth_rows = rows_here // WIN
    depth_cols = cols_here // WIN
    row_count = lax.axis_size("rows")
    col_count = lax.axis_size("cols")
    row_index = lax.axis_index("rows")
    col_index = lax.axis_index("cols")
    row_cap = (WIN + row_count - 1) // row_count
    col_cap = (WIN + col_count - 1) // col_count
    groups = spatial.reshape(WIN, depth_rows, cols_here, channels)
    outgoing = send_slots(groups, row_count, row_index).reshape(
        row_cap, row_count, depth_rows, cols_here, channels
    )
    arrived = lax.all_to_all(outgoing, "rows", split_axis=1, concat_axis=1, tiled=True)
    arrived = arrived.reshape(row_cap * row_count, depth_rows, cols_here, channels)
    strips = receive_slots(arrived, row_count, row_index)
    strips = strips.reshape(WIN, depth_rows, WIN, depth_cols, channels).transpose(2, 0, 1, 3, 4)
    outgoing = send_slots(strips, col_count, col_index)
    outgoing = outgoing.reshape(col_cap, col_count, WIN, depth_rows, depth_cols, channels)
    arrived = lax.all_to_all(outgoing, "cols", split_axis=1, concat_axis=1, tiled=True)
    arrived = arrived.reshape(col_cap * col_count, WIN, depth_rows, depth_cols, channels)
    placed = receive_slots(arrived, col_count, col_index)
    return placed.transpose(2, 3, 1, 0, 4).reshape(depth_rows * depth_cols, WIN * WIN, channels)


def from_grid(windows, rows_here, cols_here):
    channels = windows.shape[-1]
    depth_rows = rows_here // WIN
    depth_cols = cols_here // WIN
    row_count = lax.axis_size("rows")
    col_count = lax.axis_size("cols")
    row_index = lax.axis_index("rows")
    col_index = lax.axis_index("cols")
    row_cap = (WIN + row_count - 1) // row_count
    col_cap = (WIN + col_count - 1) // col_count
    placed = windows.reshape(depth_rows, depth_cols, WIN, WIN, channels).transpose(3, 2, 0, 1, 4)
    outgoing = return_slots(placed, col_count, col_index)
    outgoing = outgoing.reshape(col_cap, col_count, WIN, depth_rows, depth_cols, channels)
    arrived = lax.all_to_all(outgoing, "cols", split_axis=1, concat_axis=1, tiled=True)
    arrived = arrived.reshape(col_cap * col_count, WIN, depth_rows, depth_cols, channels)
    strips = restore_slots(arrived, col_count, col_index)
    strips = strips.transpose(1, 2, 0, 3, 4).reshape(WIN, depth_rows, cols_here, channels)
    outgoing = return_slots(strips, row_count, row_index)
    outgoing = outgoing.reshape(row_cap, row_count, depth_rows, cols_here, channels)
    arrived = lax.all_to_all(outgoing, "rows", split_axis=1, concat_axis=1, tiled=True)
    arrived = arrived.reshape(row_cap * row_count, depth_rows, cols_here, channels)
    groups = restore_slots(arrived, row_count, row_index)
    return groups.reshape(rows_here, cols_here, channels)


def local(
    inputs,
    cotangent,
    conv_gain,
    expand_weight,
    depth_weight,
    project_weight,
    block_gain,
    block_qkv,
    block_out,
    block_bias,
    grid_gain,
    grid_qkv,
    grid_out,
    grid_bias,
):
    rows_here, cols_here, channels = inputs.shape

    def expand(values):
        normed = layer_norm(values, conv_gain).astype(jnp.bfloat16)
        flattened = normed.reshape(values.shape[0] * values.shape[1], channels)
        hidden = jnp.dot(flattened, expand_weight, preferred_element_type=jnp.float32)
        hidden = jax.nn.gelu(hidden, approximate=False).astype(jnp.bfloat16)
        return hidden.reshape(values.shape[0], values.shape[1], -1)

    def update_of(pre_values):
        branch = jax.nn.gelu(pre_values, approximate=False).astype(jnp.bfloat16)
        return jnp.dot(
            branch.reshape(-1, branch.shape[-1]), project_weight, preferred_element_type=jnp.float32
        )

    def mix(pre_values, values):
        update = update_of(pre_values).reshape(rows_here, cols_here, channels)
        return (values.astype(jnp.float32) + update).astype(jnp.bfloat16)

    def block_part(mixed_map):
        blocked = attend(to_blocks(mixed_map), block_gain, block_qkv, block_out, block_bias)
        return from_blocks(blocked, rows_here, cols_here)

    def local_tail(pre_values, values):
        return block_part(mix(pre_values, values))

    expanded, expand_pull = jax.vjp(expand, inputs)
    padded = with_halo(expanded, (("rows", 0), ("cols", 1)), 1)
    pre_act = depthwise(padded.astype(jnp.float32), depth_weight, rows_here, cols_here)
    blocked, tail_pull = jax.vjp(local_tail, pre_act, inputs)

    def grid_attend(windows):
        return attend(windows, grid_gain, grid_qkv, grid_out, grid_bias)

    gridded, grid_pull = jax.vjp(grid_attend, to_grid(blocked))
    result = from_grid(gridded, rows_here, cols_here)
    grad_gridded = to_grid(cotangent)
    grad_blocked = from_grid(grid_pull(grad_gridded)[0], rows_here, cols_here)
    grad_pre, grad_tail = tail_pull(grad_blocked)
    grad_padded = with_halo(grad_pre.astype(jnp.bfloat16), (("rows", 0), ("cols", 1)), 1).astype(
        grad_pre.dtype
    )
    grad_expanded = depthwise_back(grad_padded, depth_weight, rows_here, cols_here).astype(
        jnp.bfloat16
    )
    gradient = grad_tail + expand_pull(grad_expanded)[0]
    return (result, gradient)


def solution(mesh):
    in_specs = (
        P("rows", "cols", None),
        P("rows", "cols", None),
        P(),
        P(),
        P(),
        P(),
        P(),
        P(),
        P(),
        P(),
        P(),
        P(),
        P(),
        P(),
    )
    out_specs = (P("rows", "cols", None), P("rows", "cols", None))
    return jax.shard_map(local, mesh=mesh, in_specs=in_specs, out_specs=out_specs, check_vma=False)
```

profile of v0, /device:TPU:48, one launch (start us, length us, event | category | flops | bytes accessed | tf_op | source)
XLA Modules:
  0.0 383.7 jit_solution(2712046607430521789)
XLA Ops:
  4.2 5.1 %multiply_convert_fusion.1 = (bf16[196,2048]{1,0:T(8,128)(2,1)S(1)}, f32[196,2048]{1,0:T(8,128)}, f32[196,2048]{1,0:T(8,128)}) fusion(bf16[196,512]{1,0:T(8,128)(2,1)S(1)} %reshape.525, bf16[512,2048]{1,0:T(8,128)(2,1)S(1)} %copy-done), kind=kOutput, calls=%fused_computation.107 | convolution fusion | flops 437133312 | bytes 6311936 | tf_op jit(solution)/shard_map/jvp()/dot_general | solution.py:204
  12.0 7.3 %collective-permute-start.1 = (bf16[1,28,2048]{2,1,0:T(8,128)(2,1)}, bf16[1,28,2048]{2,1,0:T(8,128)(2,1)S(1)}, u32[]{:S(2)}, u32[]{:S(2)}) collective-permute-start(bf16[1,28,2048]{2,1,0:T(8,128)(2,1)} %get-tuple-element.28), channel_id=1, source_target_pairs={{8,0},{16,8},{24,16},{32,24},{40,32},{48,40},{56,48},{64,56},{72,6... | collective-permute-start | bytes 344072 | tf_op jit(solution)/shard_map/ppermute | solution.py:22
  38.6 5.6 %fusion.15 = (f32[7,28,2048]{2,1,0:T(8,128)S(1)}, f32[7,28,2048]{2,1,0:T(8,128)S(1)}) fusion(f32[2048]{0:T(1024)S(1)} %bitcast.378, f32[9,30,2048]{2,1,0:T(8,128)S(1)} %maximum_convert_fusion, f32[2048]{0:T(1024)S(1)} %bitcast.380, f32[2048]{0:T(1024)S(1)} %bitcast.366, f32[2048]{0:T(1024)S(1)} %bitcast.368, f32[2048]{0:T(1024)S(1)} %bitcast.370, ...), kind=kLoop, calls=%fused_computation.40 | loop fusion | flops 31711232 | bytes 17735680 | tf_op jit(solution)/shard_map/jvp()/erfc | solution.py:209
  82.6 5.4 %all-to-all-start.4 = ((bf16[1,16,1,28,512]{4,3,2,0,1:T(8,128)(2,1)}), bf16[1,16,1,28,512]{4,3,2,0,1:T(8,128)(2,1)}, u32[]{:S(2)}, u32[]{:S(2)}) async-start(bf16[1,16,1,28,512]{4,3,2,0,1:T(8,128)(2,1)} %get-tuple-element.45), calls=%async_computation.4 | async-start | bytes 1048576 | tf_op jit(solution)/shard_map/all_to_all | solution.py:146
  88.2 9.5 %all-to-all-done.4 = bf16[1,16,1,28,512]{4,3,2,0,1:T(8,128)(2,1)} async-done(((bf16[1,16,1,28,512]{4,3,2,0,1:T(8,128)(2,1)}), bf16[1,16,1,28,512]{4,3,2,0,1:T(8,128)(2,1)}, u32[]{:S(2)}, u32[]{:S(2)}) %all-to-all-start.4) | async-done | bytes 458784 | tf_op jit(solution)/shard_map/all_to_all | solution.py:146
  97.6 7.0 %all-to-all-start = ((bf16[1,16,1,28,512]{4,3,2,0,1:T(8,128)(2,1)}), bf16[1,16,1,28,512]{4,3,2,0,1:T(8,128)(2,1)}, u32[]{:S(2)}, u32[]{:S(2)}) async-start(bf16[1,16,1,28,512]{4,3,2,0,1:T(8,128)(2,1)} %get-tuple-element.46), calls=%async_computation | async-start | bytes 1048576 | tf_op jit(solution)/shard_map/all_to_all | solution.py:146
  106.9 7.4 %all-to-all-done = bf16[1,16,1,28,512]{4,3,2,0,1:T(8,128)(2,1)} async-done(((bf16[1,16,1,28,512]{4,3,2,0,1:T(8,128)(2,1)}), bf16[1,16,1,28,512]{4,3,2,0,1:T(8,128)(2,1)}, u32[]{:S(2)}, u32[]{:S(2)}) %all-to-all-start) | async-done | bytes 458784 | tf_op jit(solution)/shard_map/all_to_all | solution.py:146
  129.7 6.9 %all-to-all-start.1 = ((bf16[1,8,7,1,4,512]{5,4,2,3,0,1:T(4,128)(2,1)}), bf16[1,8,7,1,4,512]{5,4,2,3,0,1:T(4,128)(2,1)S(1)}, u32[]{:S(2)}, u32[]{:S(2)}) async-start(bf16[1,8,7,1,4,512]{5,4,2,3,0,1:T(4,128)(2,1)} %get-tuple-element.44), calls=%async_computation.1 | async-start | bytes 458752 | tf_op jit(solution)/shard_map/all_to_all | solution.py:152
  137.2 5.0 %all-to-all-done.1 = bf16[1,8,7,1,4,512]{5,4,2,3,0,1:T(4,128)(2,1)S(1)} async-done(((bf16[1,8,7,1,4,512]{5,4,2,3,0,1:T(4,128)(2,1)}), bf16[1,8,7,1,4,512]{5,4,2,3,0,1:T(4,128)(2,1)S(1)}, u32[]{:S(2)}, u32[]{:S(2)}) %all-to-all-start.1) | async-done | bytes 229408 | tf_op jit(solution)/shard_map/all_to_all | solution.py:152
  142.3 5.7 %all-to-all-start.5 = ((bf16[1,8,7,1,4,512]{5,4,2,3,0,1:T(4,128)(2,1)}), bf16[1,8,7,1,4,512]{5,4,2,3,0,1:T(4,128)(2,1)}, u32[]{:S(2)}, u32[]{:S(2)}) async-start(bf16[1,8,7,1,4,512]{5,4,2,3,0,1:T(4,128)(2,1)} %get-tuple-element.43), calls=%async_computation.5 | async-start | bytes 458752 | tf_op jit(solution)/shard_map/all_to_all | solution.py:152
  180.0 4.2 %fusion.224 = (f32[4,16,49]{2,1,0:T(8,128)}, f32[4,16,49,49]{2,3,1,0:T(8,128)}) fusion(f32[16,49,49]{1,2,0:T(8,128)} %copy.160, bf16[4,49,1,16,32]{1,4,3,0,2:T(8,128)(2,1)} %copy.216, bf16[4,49,1,16,32]{1,4,3,0,2:T(8,128)(2,1)} %copy.215), kind=kOutput, calls=%fused_computation.410 | convolution fusion | flops 10449200 | bytes 1182272 | tf_op jit(solution)/shard_map/jvp()/sub | solution.py:45
  234.6 5.1 %all-to-all-start.6 = ((bf16[1,8,7,1,4,512]{5,4,2,3,0,1:T(4,128)(2,1)}), bf16[1,8,7,1,4,512]{5,4,2,3,0,1:T(4,128)(2,1)S(1)}, u32[]{:S(2)}, u32[]{:S(2)}) async-start(bf16[1,8,7,1,4,512]{5,4,2,3,0,1:T(4,128)(2,1)} %get-tuple-element.41), calls=%async_computation.6 | async-start | bytes 458752 | tf_op jit(solution)/shard_map/all_to_all | solution.py:171
  239.7 5.3 %all-to-all-done.6 = bf16[1,8,7,1,4,512]{5,4,2,3,0,1:T(4,128)(2,1)S(1)} async-done(((bf16[1,8,7,1,4,512]{5,4,2,3,0,1:T(4,128)(2,1)}), bf16[1,8,7,1,4,512]{5,4,2,3,0,1:T(4,128)(2,1)S(1)}, u32[]{:S(2)}, u32[]{:S(2)}) %all-to-all-start.6) | async-done | bytes 229408 | tf_op jit(solution)/shard_map/all_to_all | solution.py:171
  245.0 5.7 %all-to-all-start.2 = ((bf16[1,8,7,1,4,512]{5,4,2,3,0,1:T(4,128)(2,1)}), bf16[1,8,7,1,4,512]{5,4,2,3,0,1:T(4,128)(2,1)}, u32[]{:S(2)}, u32[]{:S(2)}) async-start(bf16[1,8,7,1,4,512]{5,4,2,3,0,1:T(4,128)(2,1)} %get-tuple-element.42), calls=%async_computation.2 | async-start | bytes 458752 | tf_op jit(solution)/shard_map/all_to_all | solution.py:171
  252.2 4.0 %all-to-all-done.2 = bf16[1,8,7,1,4,512]{5,4,2,3,0,1:T(4,128)(2,1)} async-done(((bf16[1,8,7,1,4,512]{5,4,2,3,0,1:T(4,128)(2,1)}), bf16[1,8,7,1,4,512]{5,4,2,3,0,1:T(4,128)(2,1)}, u32[]{:S(2)}, u32[]{:S(2)}) %all-to-all-start.2) | async-done | bytes 229408 | tf_op jit(solution)/shard_map/all_to_all | solution.py:171
  271.2 6.4 %all-to-all-start.7 = ((bf16[1,16,1,28,512]{4,3,2,0,1:T(8,128)(2,1)}), bf16[1,16,1,28,512]{4,3,2,0,1:T(8,128)(2,1)}, u32[]{:S(2)}, u32[]{:S(2)}) async-start(bf16[1,16,1,28,512]{4,3,2,0,1:T(8,128)(2,1)} %get-tuple-element.39), calls=%async_computation.7 | async-start | bytes 1048576 | tf_op jit(solution)/shard_map/all_to_all | solution.py:177
  277.6 9.6 %all-to-all-done.7 = bf16[1,16,1,28,512]{4,3,2,0,1:T(8,128)(2,1)} async-done(((bf16[1,16,1,28,512]{4,3,2,0,1:T(8,128)(2,1)}), bf16[1,16,1,28,512]{4,3,2,0,1:T(8,128)(2,1)}, u32[]{:S(2)}, u32[]{:S(2)}) %all-to-all-start.7) | async-done | bytes 458784 | tf_op jit(solution)/shard_map/all_to_all | solution.py:177
  287.1 7.0 %all-to-all-start.3 = ((bf16[1,16,1,28,512]{4,3,2,0,1:T(8,128)(2,1)}), bf16[1,16,1,28,512]{4,3,2,0,1:T(8,128)(2,1)}, u32[]{:S(2)}, u32[]{:S(2)}) async-start(bf16[1,16,1,28,512]{4,3,2,0,1:T(8,128)(2,1)} %get-tuple-element.40), calls=%async_computation.3 | async-start | bytes 1048576 | tf_op jit(solution)/shard_map/all_to_all | solution.py:177
  297.1 6.7 %all-to-all-done.3 = bf16[1,16,1,28,512]{4,3,2,0,1:T(8,128)(2,1)} async-done(((bf16[1,16,1,28,512]{4,3,2,0,1:T(8,128)(2,1)}), bf16[1,16,1,28,512]{4,3,2,0,1:T(8,128)(2,1)}, u32[]{:S(2)}, u32[]{:S(2)}) %all-to-all-start.3) | async-done | bytes 458784 | tf_op jit(solution)/shard_map/all_to_all | solution.py:177
  342.5 4.9 %collective-permute-start.5 = (bf16[1,28,2048]{2,1,0:T(8,128)(2,1)S(1)}, bf16[1,28,2048]{2,1,0:T(8,128)(2,1)S(1)}, u32[]{:S(2)}, u32[]{:S(2)}) collective-permute-start(bf16[1,28,2048]{2,1,0:T(8,128)(2,1)S(1)} %get-tuple-element.27), channel_id=1, source_target_pairs={{8,0},{16,8},{24,16},{32,24},{40,32},{48,40},{56,48},{64,56},{72,6... | collective-permute-start | bytes 344072 | tf_op jit(solution)/shard_map/ppermute | solution.py:22
  349.9 7.5 %collective-permute-done.4 = bf16[1,28,2048]{2,1,0:T(8,128)(2,1)S(1)} collective-permute-done((bf16[1,28,2048]{2,1,0:T(8,128)(2,1)S(1)}, bf16[1,28,2048]{2,1,0:T(8,128)(2,1)S(1)}, u32[]{:S(2)}, u32[]{:S(2)}) %collective-permute-start.4) | collective-permute-done | bytes 114720 | tf_op jit(solution)/shard_map/ppermute | solution.py:19
  357.5 4.6 %collective-permute-start.7 = (bf16[9,1,2048]{2,1,0:T(2,128)(2,1)S(1)}, bf16[9,1,2048]{2,1,0:T(2,128)(2,1)S(1)}, u32[]{:S(2)}, u32[]{:S(2)}) collective-permute-start(bf16[9,1,2048]{2,1,0:T(2,128)(2,1)S(1)} %get-tuple-element.23), channel_id=1, source_target_pairs={{1,0},{2,1},{3,2},{4,3},{5,4},{6,5},{7,6},{9,8},{10,9},{11,10},{12... | collective-permute-start | bytes 110600 | tf_op jit(solution)/shard_map/ppermute | solution.py:22
  364.3 5.0 %collective-permute-done.6 = bf16[9,1,2048]{2,1,0:T(2,128)(2,1)S(1)} collective-permute-done((bf16[9,1,2048]{2,1,0:T(2,128)(2,1)S(1)}, bf16[9,1,2048]{2,1,0:T(2,128)(2,1)S(1)}, u32[]{:S(2)}, u32[]{:S(2)}) %collective-permute-start.6) | collective-permute-done | bytes 36896 | tf_op jit(solution)/shard_map/ppermute | solution.py:19
  376.8 4.1 %multiply_reduce_fusion.2 = (f32[196]{0:T(256)S(1)}, f32[196,512]{1,0:T(8,128)}) fusion(f32[196]{0:T(256)S(1)} %rsqrt.45, f32[512]{0:T(512)S(1)} %copy-done.35, bf16[512,2048]{1,0:T(8,128)(2,1)S(1)} %copy-done, f32[196,2048]{1,0:T(8,128)} %reshape.568, f32[196,2048]{1,0:T(8,128)} %get-tuple-element.15, f32[196,2048]{1,0:T(8,128)} %get-tuple-element.55), kind=kOutput, calls=%fused_computation.219 | convolution fusion | flops 416761664 | bytes 7319072 | tf_op jit(solution)/shard_map/transpose(jvp())/dot_general | solution.py:204
  (326 shorter events, 236.7 us)
Async XLA Ops:
  10.1 13.1 %collective-permute-start = (bf16[1,28,2048]{2,1,0:T(8,128)(2,1)S(1)}, bf16[1,28,2048]{2,1,0:T(8,128)(2,1)S(1)}, u32[]{:S(2)}, u32[]{:S(2)}) collective-permute-start(bf16[1,28,2048]{2,1,0:T(8,128)(2,1)S(1)} %get-tuple-element.29), channel_id=1, source_target_pairs={{0,8},{8,16},{16,24},{24,32},{32,40},{40,48},{48,56},{56,64},{64,7... | collective-permute-start | bytes 344072 | tf_op jit(solution)/shard_map/ppermute | solution.py:19
  12.0 11.3 %collective-permute-start.1 = (bf16[1,28,2048]{2,1,0:T(8,128)(2,1)}, bf16[1,28,2048]{2,1,0:T(8,128)(2,1)S(1)}, u32[]{:S(2)}, u32[]{:S(2)}) collective-permute-start(bf16[1,28,2048]{2,1,0:T(8,128)(2,1)} %get-tuple-element.28), channel_id=1, source_target_pairs={{8,0},{16,8},{24,16},{32,24},{40,32},{48,40},{56,48},{64,56},{72,6... | collective-permute-start | bytes 344072 | tf_op jit(solution)/shard_map/ppermute | solution.py:22
  21.2 17.4 %copy-start.18 = (f32[1,2048]{1,0:T(1,128)}, f32[1,2048]{1,0:T(1,128)S(1)}, u32[]{:S(2)}) copy-start(f32[1,2048]{1,0:T(1,128)S(1)} %get-tuple-element.33) | copy-start | bytes 24580
  21.2 17.4 %copy-start.20 = (f32[1,2048]{1,0:T(1,128)}, f32[1,2048]{1,0:T(1,128)S(1)}, u32[]{:S(2)}) copy-start(f32[1,2048]{1,0:T(1,128)S(1)} %get-tuple-element.34) | copy-start | bytes 24580
  21.2 17.4 %copy-start.22 = (f32[1,2048]{1,0:T(1,128)}, f32[1,2048]{1,0:T(1,128)S(1)}, u32[]{:S(2)}) copy-start(f32[1,2048]{1,0:T(1,128)S(1)} %get-tuple-element.35) | copy-start | bytes 24580
  21.2 17.4 %copy-start.24 = (f32[1,2048]{1,0:T(1,128)}, f32[1,2048]{1,0:T(1,128)S(1)}, u32[]{:S(2)}) copy-start(f32[1,2048]{1,0:T(1,128)S(1)} %get-tuple-element.36) | copy-start | bytes 24580
  21.2 17.4 %copy-start.26 = (f32[1,2048]{1,0:T(1,128)}, f32[1,2048]{1,0:T(1,128)S(1)}, u32[]{:S(2)}) copy-start(f32[1,2048]{1,0:T(1,128)S(1)} %get-tuple-element.37) | copy-start | bytes 24580
  24.4 12.4 %collective-permute-start.3 = (bf16[9,1,2048]{2,1,0:T(2,128)(2,1)S(1)}, bf16[9,1,2048]{2,1,0:T(2,128)(2,1)S(1)}, u32[]{:S(2)}, u32[]{:S(2)}) collective-permute-start(bf16[9,1,2048]{2,1,0:T(2,128)(2,1)S(1)} %get-tuple-element.25), channel_id=1, source_target_pairs={{1,0},{2,1},{3,2},{4,3},{5,4},{6,5},{7,6},{9,8},{10,9},{11,10},{12... | collective-permute-start | bytes 110600 | tf_op jit(solution)/shard_map/ppermute | solution.py:22
  27.2 9.6 %collective-permute-start.2 = (bf16[9,1,2048]{2,1,0:T(2,128)(2,1)S(1)}, bf16[9,1,2048]{2,1,0:T(2,128)(2,1)S(1)}, u32[]{:S(2)}, u32[]{:S(2)}) collective-permute-start(bf16[9,1,2048]{2,1,0:T(2,128)(2,1)S(1)} %get-tuple-element.24), channel_id=1, source_target_pairs={{0,1},{1,2},{2,3},{3,4},{4,5},{5,6},{6,7},{8,9},{9,10},{10,11},{11... | collective-permute-start | bytes 110600 | tf_op jit(solution)/shard_map/ppermute | solution.py:19
  80.2 25.0 %copy-start.55 = (s32[7]{0:T(128)S(1)}, s32[7]{0:T(128)}, u32[]{:S(2)}) copy-start(s32[7]{0:T(128)} %compare_select_fusion.6) | copy-start | bytes 88
  82.6 15.0 %all-to-all-start.4 = ((bf16[1,16,1,28,512]{4,3,2,0,1:T(8,128)(2,1)}), bf16[1,16,1,28,512]{4,3,2,0,1:T(8,128)(2,1)}, u32[]{:S(2)}, u32[]{:S(2)}) async-start(bf16[1,16,1,28,512]{4,3,2,0,1:T(8,128)(2,1)} %get-tuple-element.45), calls=%async_computation.4 | async-start | bytes 1048576 | tf_op jit(solution)/shard_map/all_to_all | solution.py:146
  88.1 75.6 %copy-start.48 = (pred[7]{0:T(512)(128)(4,1)}, pred[7]{0:T(512)(128)(4,1)S(1)}, u32[]{:S(2)}) copy-start(pred[7]{0:T(512)(128)(4,1)S(1)} %compare_and_fusion.4) | copy-start | bytes 25
  97.6 16.6 %all-to-all-start = ((bf16[1,16,1,28,512]{4,3,2,0,1:T(8,128)(2,1)}), bf16[1,16,1,28,512]{4,3,2,0,1:T(8,128)(2,1)}, u32[]{:S(2)}, u32[]{:S(2)}) async-start(bf16[1,16,1,28,512]{4,3,2,0,1:T(8,128)(2,1)} %get-tuple-element.46), calls=%async_computation | async-start | bytes 1048576 | tf_op jit(solution)/shard_map/all_to_all | solution.py:146
  129.7 12.5 %all-to-all-start.1 = ((bf16[1,8,7,1,4,512]{5,4,2,3,0,1:T(4,128)(2,1)}), bf16[1,8,7,1,4,512]{5,4,2,3,0,1:T(4,128)(2,1)S(1)}, u32[]{:S(2)}, u32[]{:S(2)}) async-start(bf16[1,8,7,1,4,512]{5,4,2,3,0,1:T(4,128)(2,1)} %get-tuple-element.44), calls=%async_computation.1 | async-start | bytes 458752 | tf_op jit(solution)/shard_map/all_to_all | solution.py:152
  142.3 11.1 %all-to-all-start.5 = ((bf16[1,8,7,1,4,512]{5,4,2,3,0,1:T(4,128)(2,1)}), bf16[1,8,7,1,4,512]{5,4,2,3,0,1:T(4,128)(2,1)}, u32[]{:S(2)}, u32[]{:S(2)}) async-start(bf16[1,8,7,1,4,512]{5,4,2,3,0,1:T(4,128)(2,1)} %get-tuple-element.43), calls=%async_computation.5 | async-start | bytes 458752 | tf_op jit(solution)/shard_map/all_to_all | solution.py:152
  234.6 10.5 %all-to-all-start.6 = ((bf16[1,8,7,1,4,512]{5,4,2,3,0,1:T(4,128)(2,1)}), bf16[1,8,7,1,4,512]{5,4,2,3,0,1:T(4,128)(2,1)S(1)}, u32[]{:S(2)}, u32[]{:S(2)}) async-start(bf16[1,8,7,1,4,512]{5,4,2,3,0,1:T(4,128)(2,1)} %get-tuple-element.41), calls=%async_computation.6 | async-start | bytes 458752 | tf_op jit(solution)/shard_map/all_to_all | solution.py:171
  245.0 11.2 %all-to-all-start.2 = ((bf16[1,8,7,1,4,512]{5,4,2,3,0,1:T(4,128)(2,1)}), bf16[1,8,7,1,4,512]{5,4,2,3,0,1:T(4,128)(2,1)}, u32[]{:S(2)}, u32[]{:S(2)}) async-start(bf16[1,8,7,1,4,512]{5,4,2,3,0,1:T(4,128)(2,1)} %get-tuple-element.42), calls=%async_computation.2 | async-start | bytes 458752 | tf_op jit(solution)/shard_map/all_to_all | solution.py:171
  268.8 26.6 %copy-start.33 = (f32[4,16,49]{2,1,0:T(8,128)S(1)}, f32[4,16,49]{2,1,0:T(8,128)}, u32[]{:S(2)}) copy-start(f32[4,16,49]{2,1,0:T(8,128)} %copy-done.32) | copy-start | bytes 37636
  271.2 15.9 %all-to-all-start.7 = ((bf16[1,16,1,28,512]{4,3,2,0,1:T(8,128)(2,1)}), bf16[1,16,1,28,512]{4,3,2,0,1:T(8,128)(2,1)}, u32[]{:S(2)}, u32[]{:S(2)}) async-start(bf16[1,16,1,28,512]{4,3,2,0,1:T(8,128)(2,1)} %get-tuple-element.39), calls=%async_computation.7 | async-start | bytes 1048576 | tf_op jit(solution)/shard_map/all_to_all | solution.py:177
  287.1 16.6 %all-to-all-start.3 = ((bf16[1,16,1,28,512]{4,3,2,0,1:T(8,128)(2,1)}), bf16[1,16,1,28,512]{4,3,2,0,1:T(8,128)(2,1)}, u32[]{:S(2)}, u32[]{:S(2)}) async-start(bf16[1,16,1,28,512]{4,3,2,0,1:T(8,128)(2,1)} %get-tuple-element.40), calls=%async_computation.3 | async-start | bytes 1048576 | tf_op jit(solution)/shard_map/all_to_all | solution.py:177
  342.5 7.4 %collective-permute-start.5 = (bf16[1,28,2048]{2,1,0:T(8,128)(2,1)S(1)}, bf16[1,28,2048]{2,1,0:T(8,128)(2,1)S(1)}, u32[]{:S(2)}, u32[]{:S(2)}) collective-permute-start(bf16[1,28,2048]{2,1,0:T(8,128)(2,1)S(1)} %get-tuple-element.27), channel_id=1, source_target_pairs={{8,0},{16,8},{24,16},{32,24},{40,32},{48,40},{56,48},{64,56},{72,6... | collective-permute-start | bytes 344072 | tf_op jit(solution)/shard_map/ppermute | solution.py:22
  347.4 10.0 %collective-permute-start.4 = (bf16[1,28,2048]{2,1,0:T(8,128)(2,1)S(1)}, bf16[1,28,2048]{2,1,0:T(8,128)(2,1)S(1)}, u32[]{:S(2)}, u32[]{:S(2)}) collective-permute-start(bf16[1,28,2048]{2,1,0:T(8,128)(2,1)S(1)} %get-tuple-element.26), channel_id=1, source_target_pairs={{0,8},{8,16},{16,24},{24,32},{32,40},{40,48},{48,56},{56,64},{64,7... | collective-permute-start | bytes 344072 | tf_op jit(solution)/shard_map/ppermute | solution.py:19
  357.5 6.8 %collective-permute-start.7 = (bf16[9,1,2048]{2,1,0:T(2,128)(2,1)S(1)}, bf16[9,1,2048]{2,1,0:T(2,128)(2,1)S(1)}, u32[]{:S(2)}, u32[]{:S(2)}) collective-permute-start(bf16[9,1,2048]{2,1,0:T(2,128)(2,1)S(1)} %get-tuple-element.23), channel_id=1, source_target_pairs={{1,0},{2,1},{3,2},{4,3},{5,4},{6,5},{7,6},{9,8},{10,9},{11,10},{12... | collective-permute-start | bytes 110600 | tf_op jit(solution)/shard_map/ppermute | solution.py:22
  362.1 7.1 %collective-permute-start.6 = (bf16[9,1,2048]{2,1,0:T(2,128)(2,1)S(1)}, bf16[9,1,2048]{2,1,0:T(2,128)(2,1)S(1)}, u32[]{:S(2)}, u32[]{:S(2)}) collective-permute-start(bf16[9,1,2048]{2,1,0:T(2,128)(2,1)S(1)} %get-tuple-element.22), channel_id=1, source_target_pairs={{0,1},{1,2},{2,3},{3,4},{4,5},{5,6},{6,7},{8,9},{9,10},{10,11},{11... | collective-permute-start | bytes 110600 | tf_op jit(solution)/shard_map/ppermute | solution.py:19
  (50 other events, 271.6 us)
where the time goes:
time: 391 us; the launch traced here: 384 us
  local copies, waits for them, and re-layouts  134 us (34%)
  starting transfers between devices  78 us (20%)
  waiting for transfers between devices  63.6 us (16%)
  matrix products  55.8 us (14%)
  other arithmetic  49.7 us (13%)
    unnamed x126, local copies, waits for them, and re-layouts  24.1 us
    ppermute x4, starting transfers between devices, with_halo(): lax.ppermute(lax.slice_in_dim(block, 0, width, axis=dim), axis, backward)  19.5 us
    all_to_all x2, waiting for transfers between devices, to_grid(): lax.all_to_all(outgoing, 'rows', split_axis=1, concat_axis=1, tiled=True)  16.8 us
    all_to_all x2, waiting for transfers between devices, from_grid(): lax.all_to_all(outgoing, 'rows', split_axis=1, concat_axis=1, tiled=True)  16.3 us
    reshape x4, local copies, waits for them, and re-layouts, attend(): packed = packed.reshape(window_count, length, 3, HEADS, HEAD_DIM)  15.1 us
    gather x8, local copies, waits for them, and re-layouts, pick_groups(): jnp.take(blocks, jnp.minimum(group_ids, blocks.shape[0] - 1), axis=0)  14.2 us
    all_to_all x2, starting transfers between devices, from_grid(): lax.all_to_all(outgoing, 'rows', split_axis=1, concat_axis=1, tiled=True)  13.4 us
    dot_general x4, matrix products, attend(): jnp.dot(normed, qkv_weight, preferred_element_type=jnp.float32)  12.6 us
  transfers between devices with their start and end apart: 16, of which 11 were waited for; matrix products, arithmetic and copies ran while one was open for 5% of the time, Pallas kernels for 0%

commit v1 on v0

v1 whole, which is shorter than its diff:
```python
import functools

import jax
import jax.numpy as jnp
import numpy as np
from jax import lax
from jax.experimental import pallas as pl
from jax.experimental.pallas import tpu as pltpu
from jax.sharding import PartitionSpec as P

ROWS, COLS = 16, 8
HEIGHT, BREADTH = 112, 224
WIN = 7
D = 512
FF = 2048
HEAD_DIM = 32
TR, TC = 7, 28
SW = 32
NWIN, WPAD = 4, 64
LEN = 49
CHUNK = 256
EPSILON = 1e-05
F32, BF16 = jnp.float32, jnp.bfloat16
MESH = pl.DeviceIdType.MESH


def win_row(row, col):
    return WPAD * (col // WIN) + WIN * row + col % WIN


def placements():
    halo = np.zeros((352, 448))
    for rho in range(11):
        for kappa in range(32):
            r, c = rho - 2, kappa - 2
            if 0 <= r < 7:
                if 0 <= c < 28:
                    at = 32 * r + c
                elif c < 0:
                    at = 352 + 2 * r + c + 2
                else:
                    at = 368 + 2 * r + c - 28
            elif r < 0:
                if 0 <= c < 28:
                    at = 224 + 32 * (r + 2) + c
                elif c < 0:
                    at = 384 + 2 * (r + 7) + c + 2
                else:
                    at = 400 + 2 * (r + 7) + c - 28
            else:
                if 0 <= c < 28:
                    at = 288 + 32 * (r - 7) + c
                elif c < 0:
                    at = 416 + 2 * (r - 7) + c + 2
                else:
                    at = 432 + 2 * (r - 7) + c - 28
            halo[32 * rho + kappa, at] = 1
    edge = np.zeros((32, 448))
    for r in range(7):
        for c in range(2):
            edge[2 * r + c, 32 * r + c] = 1
            edge[16 + 2 * r + c, 32 * r + 26 + c] = 1
    to_win = np.zeros((256, 448))
    from_win = np.zeros((208, 448))
    back_win = np.zeros((256, 448))
    for r in range(7):
        for c in range(28):
            to_win[win_row(r, c), 32 * r + c + 2] = 1
            from_win[28 * r + c, win_row(r, c)] = 1
            back_win[win_row(r, c), 28 * r + c] = 1
    edge2 = np.zeros((96, 448))
    for c in range(28):
        edge2[c, win_row(0, c)] = 1
        edge2[32 + c, win_row(6, c)] = 1
    for r in range(7):
        edge2[64 + r, win_row(r, 0)] = 1
        edge2[80 + r, win_row(r, 27)] = 1
    halo2 = np.zeros((288, 448))
    for rho in range(9):
        for kappa in range(1, 31):
            r, c = rho - 1, kappa - 2
            if 0 <= r < 7:
                if 0 <= c < 28:
                    at = win_row(r, c)
                elif c < 0:
                    at = 320 + r
                else:
                    at = 336 + r
            elif r < 0:
                at = 256 + c if 0 <= c < 28 else (352 + 6 if c < 0 else 368 + 6)
            else:
                at = 288 + c if 0 <= c < 28 else (384 if c < 0 else 400)
            halo2[32 * rho + kappa, at] = 1
    parts = dict(
        halo=halo, edge=edge, to_win=to_win, from_win=from_win, back_win=back_win,
        edge2=edge2, halo2=halo2,
    )
    starts, at = {}, 0
    for name, part in parts.items():
        starts[name] = (at, part.shape[0])
        at += part.shape[0]
    return np.concatenate(list(parts.values())), starts


PLACES, STARTS = placements()


def dot(a, b):
    return jnp.dot(a, b, preferred_element_type=F32)


def dot_nt(a, b):
    return lax.dot_general(a, b, (((1,), (1,)), ((), ())), preferred_element_type=F32)


def dot_tn(a, b):
    return lax.dot_general(a, b, (((0,), (0,)), ((), ())), preferred_element_type=F32)


def tail(u):
    d = 1.0 + (0.3275911 * 0.5**0.5) * jnp.abs(u)
    t = pl.reciprocal(d, approx=True)
    t = t * (2.0 - d * t)
    gauss = jnp.exp(-0.5 * (u * u))
    poly = 0.5 * 1.061405429
    for coefficient in (-1.453152027, 1.421413741, -0.284496736, 0.254829592):
        poly = poly * t + 0.5 * coefficient
    return poly * t * gauss, gauss


def gelu_of(u, half):
    return jnp.maximum(u, 0.0) - jnp.abs(u) * half


def slope_of(u, half, gauss):
    return jnp.where(u >= 0.0, 1.0 - half, half) + u * gauss * (0.5 / np.pi) ** 0.5


def standardize(x):
    center = jnp.mean(x, axis=-1, keepdims=True)
    moved = x - center
    spread = jnp.mean(moved * moved, axis=-1, keepdims=True)
    scale = lax.rsqrt(spread + EPSILON)
    return moved * scale, scale


def standardize_back(grad, xhat, scale):
    first = jnp.mean(grad, axis=-1, keepdims=True)
    second = jnp.mean(grad * xhat, axis=-1, keepdims=True)
    return scale * (grad - first - xhat * second)


def by_head(x):
    head = lax.broadcasted_iota(jnp.int32, x.shape, 1) // HEAD_DIM
    zero = jnp.zeros_like(x)
    return jnp.concatenate([jnp.where(head == h, x, zero) for h in range(4)], axis=0)


def own_head(x):
    head = lax.broadcasted_iota(jnp.int32, (WPAD, 128), 1) // HEAD_DIM
    out = x[0:WPAD]
    for h in range(1, 4):
        out = jnp.where(head == h, x[WPAD * h : WPAD * (h + 1)], out)
    return out


def kernel(
    x_ref, cot_ref, cgain_ref, dw_ref, bgain_ref, ggain_ref,
    places_hbm, we_hbm, wp_hbm, bqkv_hbm, bout_hbm, bbias_hbm, gqkv_hbm, gout_hbm, gbias_hbm,
    out_ref, grad_ref,
    places, we, wp, bqkv, bout, bbias, gqkv, gout, gbias, load_sem,
    stage, cat, edges, cat2, edges2, halo_sem, halo2_sem,
    cot_send, cot_recv, fwd_send, fwd_recv, res_send, res_recv, gra_send, gra_recv, grid_sem,
    mixbuf, xhat0, scale0, normed0, slope_u, slope_p, update,
    bias_b, bias_g, zwin, packed_b, xhat_b, scale_b, prob_b, att,
    zgrid, dgrid, packed_g, xhat_g, scale_g, prob_g, dout, da, dpk, gslot,
):
    i, j = lax.axis_index("rows"), lax.axis_index("cols")
    me = i * COLS + j

    def load(index, src, dst):
        return pltpu.make_async_copy(src, dst, load_sem.at[index])

    loads = [
        load(n, src, dst)
        for n, (src, dst) in enumerate(
            [
                (places_hbm, places), (we_hbm, we), (wp_hbm, wp), (bbias_hbm, bbias),
                (gbias_hbm, gbias), (bqkv_hbm, bqkv), (bout_hbm, bout),
                (gout_hbm, gout), (gqkv_hbm, gqkv),
            ]
        )
    ]
    for one in loads:
        one.start()
    l_places, l_we, l_wp, l_bb, l_gb, l_bqkv, l_bout, l_gout, l_gqkv = loads

    barrier = pltpu.get_barrier_semaphore()

    def greet(step, carry):
        other = lax.rem(me + step, ROWS * COLS)
        pl.semaphore_signal(
            barrier, inc=1, device_id=(lax.div(other, COLS), lax.rem(other, COLS)),
            device_id_type=MESH,
        )
        return carry

    lax.fori_loop(1, ROWS * COLS, greet, 0)

    def place(name, source):
        at, size = STARTS[name]
        return dot(places[at : at + size, 0 : source.shape[0]], source)

    stage[...] = jnp.zeros_like(stage)
    for r in range(TR):
        stage[SW * r : SW * r + TC, :] = x_ref[r].astype(F32)
    cat[0:224, :] = stage[0:224, :].astype(BF16)
    l_places.wait()
    edges[...] = place("edge", cat[0:224, :]).astype(BF16)

    mixbuf[...] = jnp.zeros_like(mixbuf)
    for r in range(TR):
        for k in range(4):
            mixbuf[pl.ds(112 * r + k, TC, stride=4), :] = cot_ref[
                r, :, 128 * k : 128 * (k + 1)
            ].astype(F32)
    cot_send[...] = mixbuf[0:784, :].reshape(LEN, 16, 128).astype(BF16)

    pl.semaphore_wait(barrier, ROWS * COLS - 1)

    north, south = lax.rem(i + ROWS - 1, ROWS), lax.rem(i + 1, ROWS)
    west, east = lax.rem(j + COLS - 1, COLS), lax.rem(j + 1, COLS)

    def swap(sems, parts):
        copies = [
            pltpu.make_async_remote_copy(
                src_ref=src, dst_ref=dst, send_sem=sems.at[0, n], recv_sem=sems.at[1, n],
                device_id=to, device_id_type=MESH,
            )
            for n, (src, dst, to) in enumerate(parts)
        ]
        for one in copies:
            one.start()
        return copies

    w_cols, e_cols = edges.at[pl.ds(0, 16)], edges.at[pl.ds(16, 16)]
    halo = swap(
        halo_sem,
        [
            (cat.at[pl.ds(0, 64)], cat.at[pl.ds(288, 64)], (north, j)),
            (cat.at[pl.ds(160, 64)], cat.at[pl.ds(224, 64)], (south, j)),
            (e_cols, cat.at[pl.ds(352, 16)], (i, east)),
            (w_cols, cat.at[pl.ds(368, 16)], (i, west)),
            (e_cols, cat.at[pl.ds(384, 16)], (south, east)),
            (w_cols, cat.at[pl.ds(400, 16)], (south, west)),
            (e_cols, cat.at[pl.ds(416, 16)], (north, east)),
            (w_cols, cat.at[pl.ds(432, 16)], (north, west)),
        ],
    )

    def send_chunks(send, recv, sems, forward):
        def body(c, carry):
            a, b = lax.div(c, WIN), lax.rem(c, WIN)
            if forward:
                row, col = WIN * i + a, WIN * j + b
                ti, tj = lax.rem(row, ROWS), lax.rem(col, COLS)
                slot = lax.div(row, ROWS) * WIN + lax.div(col, COLS)
            else:
                row, col = ROWS * a + i, COLS * b + j
                ti, tj = lax.div(row, WIN), lax.div(col, WIN)
                slot = lax.rem(row, WIN) * WIN + lax.rem(col, WIN)
            mine = jnp.logical_and(ti == i, tj == j)

            @pl.when(mine)
            def _():
                pltpu.make_async_copy(send.at[c], recv.at[slot], sems.at[1]).start()

            @pl.when(jnp.logical_not(mine))
            def _():
                pltpu.make_async_remote_copy(
                    src_ref=send.at[c], dst_ref=recv.at[slot], send_sem=sems.at[0],
                    recv_sem=sems.at[1], device_id=(ti, tj), device_id_type=MESH,
                ).start()

            return carry

        lax.fori_loop(0, LEN, body, 0)

    def wait_chunks(recv, sems):
        pltpu.make_async_copy(recv, recv, sems.at[1]).wait()

    def wait_sent(send, sems):
        some = lax.rem(10 * i, ROWS) < WIN

        @pl.when(some)
        def _():
            part = send.at[pl.ds(0, LEN - 1)]
            pltpu.make_async_copy(part, part, sems.at[0]).wait()

        @pl.when(jnp.logical_not(some))
        def _():
            pltpu.make_async_copy(send, send, sems.at[0]).wait()

    send_chunks(cot_send, cot_recv, grid_sem.at[0], True)

    def flip(bias, bias_t, h):
        square = jnp.concatenate(
            [bias[h], jnp.zeros((LEN, 128 - LEN), F32)], axis=1
        )
        square = jnp.concatenate([square, jnp.zeros((WPAD - LEN, 128), F32)], axis=0)
        turned = square.T[0:WPAD]
        key = lax.broadcasted_iota(jnp.int32, (WPAD, WPAD), 0)
        return jnp.where(key < LEN, turned, -1e30)

    def flip_all(bias, bias_t):
        for g in range(4):
            for h in range(2):
                pair = [flip(bias, bias_t, 4 * g + 2 * h + n) for n in range(2)]
                bias_t[g, :, 128 * h : 128 * (h + 1)] = jnp.concatenate(pair, axis=1)

    l_bb.wait()
    flip_all(bbias, bias_b)
    l_gb.wait()
    flip_all(gbias, bias_g)

    for one in halo:
        one.wait_recv()

    def inside(count, row_shift):
        slot = lax.broadcasted_iota(jnp.int32, (count, 1), 0)
        row = TR * i + lax.shift_right_logical(slot, 5) - row_shift
        col = TC * j + lax.bitwise_and(slot, 31) - 2
        return (row >= 0) & (row < HEIGHT) & (col >= 0) & (col < BREADTH)

    xh = jnp.where(inside(352, 2), place("halo", cat[...]), 0.0)
    xhat, scale = standardize(xh)
    xhat0[...] = xhat[64:288]
    scale0[...] = scale[64:288]
    stage[0:224, :] = xh[64:288]
    normed0[...] = (xhat * cgain_ref[...]).astype(BF16)
    update[...] = jnp.zeros_like(update)
    l_we.wait()
    l_wp.wait()

    def taps(at):
        return [dw_ref[n : n + 1, pl.ds(at, CHUNK)] for n in range(9)]

    def mbconv(step, carry):
        at = pl.multiple_of(step * CHUNK, CHUNK)
        u = dot(normed0[...], we[:, pl.ds(at, CHUNK)])
        half, gauss = tail(u)
        slope_u[:, pl.ds(at, CHUNK)] = slope_of(u, half, gauss)[64:288]
        e = gelu_of(u, half).astype(BF16).astype(F32)
        w = taps(at)
        y = [sum(e[SW * a : SW * a + 288] * w[3 * a + b] for a in range(3)) for b in range(3)]
        pre = pltpu.roll(y[0], 1, 0) + y[1] + pltpu.roll(y[2], 287, 0)
        half, gauss = tail(pre)
        slope_p[:, pl.ds(at, CHUNK)] = slope_of(pre, half, gauss)
        branch = gelu_of(pre[32:256], half[32:256]).astype(BF16)
        update[...] += dot(branch, wp[pl.ds(at, CHUNK), :])
        return carry

    lax.fori_loop(0, FF // CHUNK, mbconv, 0)
    mixed = (stage[0:224, :] + update[...]).astype(BF16)
    zwin[...] = place("to_win", mixed)

    root = HEAD_DIM**-0.5

    def project_in(z, gain_ref, qkv, packed, xhat_ref, scale_ref):
        xhat, scale = standardize(z)
        xhat_ref[...] = xhat
        scale_ref[...] = scale
        normed = (xhat * gain_ref[...]).astype(BF16)
        for n in range(3):
            at = n * 512
            packed[:, at : at + 512] = dot(normed, qkv[:, at : at + 512]).astype(BF16)

    def parts_of(packed, rows, g):
        return [packed[rows, 512 * n + 128 * g : 512 * n + 128 * (g + 1)] for n in range(3)]

    def attend(packed, bias_t, prob):
        def window(w, carry):
            rows = pl.ds(pl.multiple_of(w * WPAD, WPAD), WPAD)
            for g in range(4):
                q, k, v = parts_of(packed, rows, g)
                s = dot_nt(k, by_head(q)) * root + bias_t[g]
                e = jnp.exp(s - jnp.max(s, axis=0, keepdims=True))
                p = e * (1.0 / jnp.sum(e, axis=0, keepdims=True))
                prob[w, g] = p
                att[rows, 128 * g : 128 * (g + 1)] = own_head(dot_tn(p.astype(BF16), v)).astype(
                    BF16
                )
            return carry

        lax.fori_loop(0, NWIN, window, 0)

    def attend_back(packed, prob):
        def window(w, carry):
            rows = pl.ds(pl.multiple_of(w * WPAD, WPAD), WPAD)
            for g in range(4):
                q, k, v = parts_of(packed, rows, g)
                p = prob[w, g]
                dam = by_head(da[rows, 128 * g : 128 * (g + 1)])
                dp = dot_nt(v, dam).astype(BF16).astype(F32)
                ds = p * (dp - jnp.sum(p * dp, axis=0, keepdims=True))
                ds = ds.astype(BF16)
                dq = own_head(dot_tn(ds, k)) * root
                dk = dot(ds, by_head(q)) * root
                dv = dot(p.astype(BF16), dam)
                for n, one in enumerate((dq, dk, dv)):
                    dpk[rows, 512 * n + 128 * g : 512 * n + 128 * (g + 1)] = one.astype(BF16)
            return carry

        lax.fori_loop(0, NWIN, window, 0)

    def project_back(qkv, gain_ref, xhat_ref, scale_ref):
        dn = dot_nt(dpk[...], qkv[...]).astype(BF16).astype(F32)
        dx = standardize_back(dn * gain_ref[...], xhat_ref[...], scale_ref[...])
        return (dout[...].astype(F32) + dx.astype(BF16).astype(F32)).astype(BF16)

    l_bqkv.wait()
    project_in(zwin[...], bgain_ref, bqkv, packed_b, xhat_b, scale_b)
    attend(packed_b, bias_b, prob_b)
    l_bout.wait()
    blocked = (zwin[...] + dot(att[...], bout[...])).astype(BF16)

    spatial = place("from_win", blocked)
    for k in range(4):
        mixbuf[pl.ds(k, 208, stride=4), :] = spatial[:, 128 * k : 128 * (k + 1)]
    fwd_send[...] = mixbuf[0:784, :].reshape(LEN, 16, 128).astype(BF16)
    send_chunks(fwd_send, fwd_recv, grid_sem.at[1], True)

    def to_windows(recv, target):
        mixbuf[0:784, :] = recv[...].astype(F32).reshape(784, 128)
        for w in range(NWIN):
            for k in range(4):
                target[WPAD * w : WPAD * w + LEN, 128 * k : 128 * (k + 1)] = mixbuf[
                    pl.ds(4 * w + k, LEN, stride=16), :
                ]

    def from_windows(source, send):
        for w in range(NWIN):
            for k in range(4):
                mixbuf[pl.ds(4 * w + k, LEN, stride=16), :] = source[
                    WPAD * w : WPAD * w + LEN, 128 * k : 128 * (k + 1)
                ]
        send[...] = mixbuf[0:784, :].reshape(LEN, 16, 128).astype(BF16)

    dgrid[...] = jnp.zeros_like(dgrid)
    zgrid[...] = jnp.zeros_like(zgrid)
    wait_chunks(cot_recv, grid_sem.at[0])
    to_windows(cot_recv, dgrid)
    dout[...] = dgrid[...].astype(BF16)
    l_gout.wait()
    da[...] = dot_nt(dout[...], gout[...]).astype(BF16)
    l_gqkv.wait()

    wait_chunks(fwd_recv, grid_sem.at[1])
    to_windows(fwd_recv, zgrid)
    project_in(zgrid[...], ggain_ref, gqkv, packed_g, xhat_g, scale_g)
    attend(packed_g, bias_g, prob_g)
    attend_back(packed_g, prob_g)
    dgrid[...] = project_back(gqkv, ggain_ref, xhat_g, scale_g).astype(F32)
    from_windows(dgrid, gra_send)
    send_chunks(gra_send, gra_recv, grid_sem.at[3], False)
    zgrid[...] = (zgrid[...] + dot(att[...], gout[...])).astype(BF16).astype(F32)
    from_windows(zgrid, res_send)
    send_chunks(res_send, res_recv, grid_sem.at[2], False)

    wait_chunks(gra_recv, grid_sem.at[3])
    mixbuf[0:784, :] = gra_recv[...].astype(F32).reshape(784, 128)
    mixbuf[784:832, :] = jnp.zeros((48, 128), F32)
    spatial = jnp.concatenate([mixbuf[pl.ds(k, 208, stride=4), :] for k in range(4)], axis=1)
    dout[...] = place("back_win", spatial.astype(BF16)).astype(BF16)
    da[...] = dot_nt(dout[...], bout[...]).astype(BF16)
    attend_back(packed_b, prob_b)
    cat2[0:256, :] = project_back(bqkv, bgain_ref, xhat_b, scale_b)
    edges2[...] = place("edge2", cat2[0:256, :]).astype(BF16)
    w_col2, e_col2 = edges2.at[pl.ds(64, 16)], edges2.at[pl.ds(80, 16)]
    halo2 = swap(
        halo2_sem,
        [
            (edges2.at[pl.ds(0, 32)], cat2.at[pl.ds(288, 32)], (north, j)),
            (edges2.at[pl.ds(32, 32)], cat2.at[pl.ds(256, 32)], (south, j)),
            (e_col2, cat2.at[pl.ds(320, 16)], (i, east)),
            (w_col2, cat2.at[pl.ds(336, 16)], (i, west)),
            (e_col2, cat2.at[pl.ds(352, 16)], (south, east)),
            (w_col2, cat2.at[pl.ds(368, 16)], (south, west)),
            (e_col2, cat2.at[pl.ds(384, 16)], (north, east)),
            (w_col2, cat2.at[pl.ds(400, 16)], (north, west)),
        ],
    )

    wait_chunks(res_recv, grid_sem.at[2])
    mixbuf[0:784, :] = res_recv[...].astype(F32).reshape(784, 128)
    for r in range(TR):
        for k in range(4):
            out_ref[r, :, 128 * k : 128 * (k + 1)] = mixbuf[
                pl.ds(112 * r + k, TC, stride=4), :
            ].astype(BF16)

    for one in halo2:
        one.wait_recv()
    gm = jnp.where(inside(288, 1), place("halo2", cat2[...]), 0.0)
    stage[0:224, :] = gm[32:256]
    gslot[...] = gm.astype(BF16)
    update[...] = jnp.zeros_like(update)

    def mbconv_back(step, carry):
        at = pl.multiple_of(step * CHUNK, CHUNK)
        gp = dot_nt(gslot[...], wp[pl.ds(at, CHUNK), :]).astype(BF16).astype(F32)
        gp = gp * slope_p[:, pl.ds(at, CHUNK)]
        w = taps(at)
        y = [
            sum(gp[SW * (2 - a) : SW * (2 - a) + 224] * w[3 * a + b] for a in range(3))
            for b in range(3)
        ]
        ge = pltpu.roll(y[0], 223, 0) + y[1] + pltpu.roll(y[2], 1, 0)
        gh = ge.astype(BF16).astype(F32) * slope_u[:, pl.ds(at, CHUNK)]
        update[...] += dot_nt(gh.astype(BF16), we[:, pl.ds(at, CHUNK)])
        return carry

    lax.fori_loop(0, FF // CHUNK, mbconv_back, 0)
    dn = update[...].astype(BF16).astype(F32)
    dx = standardize_back(dn * cgain_ref[...], xhat0[...], scale0[...])
    stage[0:224, :] = stage[0:224, :] + dx.astype(BF16).astype(F32)
    for r in range(TR):
        grad_ref[r] = stage[SW * r + 2 : SW * r + 2 + TC, :].astype(BF16)

    for one in halo + halo2:
        one.wait_send()
    for n, send in enumerate((cot_send, fwd_send, res_send, gra_send)):
        wait_sent(send, grid_sem.at[n])


def local(
    inputs, cotangent, conv_gain, expand_weight, depth_weight, project_weight,
    block_gain, block_qkv, block_out, block_bias, grid_gain, grid_qkv, grid_out, grid_bias,
):
    vmem, hbm = pl.BlockSpec(memory_space=pltpu.VMEM), pl.BlockSpec(memory_space=pl.ANY)
    places = jnp.asarray(PLACES, BF16)
    chunks = pltpu.VMEM((LEN, 16, 128), BF16)
    tokens = jax.ShapeDtypeStruct((TR, TC, D), BF16)
    bias = pltpu.VMEM((16, LEN, LEN), F32)
    bias_t = pltpu.VMEM((4, WPAD, 256), F32)
    win_f32, win_bf16 = pltpu.VMEM((256, D), F32), pltpu.VMEM((256, D), BF16)
    packed = pltpu.VMEM((256, 3 * D), BF16)
    scale = pltpu.VMEM((256, 1), F32)
    prob = pltpu.VMEM((NWIN, 4, WPAD, 256), F32)
    scratch = [
        pltpu.VMEM(PLACES.shape, BF16), pltpu.VMEM((D, FF), BF16), pltpu.VMEM((FF, D), BF16),
        pltpu.VMEM((D, 3 * D), BF16), pltpu.VMEM((D, D), BF16), bias,
        pltpu.VMEM((D, 3 * D), BF16), pltpu.VMEM((D, D), BF16), bias,
        pltpu.SemaphoreType.DMA((9,)),
        pltpu.VMEM((224, D), F32), pltpu.VMEM((448, D), BF16), pltpu.VMEM((32, D), BF16),
        pltpu.VMEM((416, D), BF16), pltpu.VMEM((96, D), BF16),
        pltpu.SemaphoreType.DMA((2, 8)), pltpu.SemaphoreType.DMA((2, 8)),
        chunks, chunks, chunks, chunks, chunks, chunks, chunks, chunks,
        pltpu.SemaphoreType.DMA((4, 2)),
        pltpu.VMEM((832, 128), F32), pltpu.VMEM((224, D), F32), pltpu.VMEM((224, 1), F32),
        pltpu.VMEM((352, D), BF16), pltpu.VMEM((224, FF), F32), pltpu.VMEM((288, FF), F32),
        pltpu.VMEM((224, D), F32),
        bias_t, bias_t, win_f32, packed, win_f32, scale, prob, win_bf16,
        win_f32, win_f32, packed, win_f32, scale, prob, win_bf16, win_bf16, packed,
        pltpu.VMEM((288, D), BF16),
    ]
    return pl.pallas_call(
        kernel,
        out_shape=(tokens, tokens),
        in_specs=[vmem] * 6 + [hbm] * 9,
        out_specs=(vmem, vmem),
        scratch_shapes=scratch,
        compiler_params=pltpu.CompilerParams(
            collective_id=0, has_side_effects=True, vmem_limit_bytes=56 * 2**20
        ),
        name="mbconv_attention",
    )(
        inputs, cotangent, conv_gain.reshape(1, D), depth_weight, block_gain.reshape(1, D),
        grid_gain.reshape(1, D), places, expand_weight, project_weight, block_qkv, block_out,
        block_bias, grid_qkv, grid_out, grid_bias,
    )


def solution(mesh):
    tokens = P("rows", "cols", None)
    in_specs = (tokens, tokens) + (P(),) * 12
    return jax.shard_map(
        local, mesh=mesh, in_specs=in_specs, out_specs=(tokens, tokens), check_vma=False
    )
```

time: 391 us -> 80.9 us (0.21)
  the two profiles are of different devices: /device:TPU:48 before, /device:TPU:0 now
where the time goes in v1:
time: 80.9 us; the launch traced here: 80.6 us
  Pallas kernels  72.9 us (90%)
  local copies, waits for them, and re-layouts  7.1 us (9%)
    pallas_call x1, Pallas kernels, local(): pl.pallas_call(kernel, out_shape=(tokens, tokens), in_specs=[vmem] * 6 +...  72.9 us
    unnamed x4, local copies, waits for them, and re-layouts  7.1 us

profile of v1, /device:TPU:0, one launch (start us, length us, event | category | flops | bytes accessed | tf_op | source)
XLA Modules:
  0.0 80.6 jit_solution(16069880946272568175)
XLA Ops:
  0.6 1.9 %copy.17.bbias_hbm = f32[16,49,49]{2,1,0:T(8,128)} copy(f32[16,49,49]{2,0,1:T(8,128)} %param.24) | data formatting | bytes 307328 | tf_op args[9]
  2.5 1.9 %copy.18.gbias_hbm = f32[16,49,49]{2,1,0:T(8,128)} copy(f32[16,49,49]{2,0,1:T(8,128)} %param.28) | data formatting | bytes 307328 | tf_op args[13]
  4.5 72.9 %mbconv_attention.1 = (bf16[7,28,512]{2,1,0:T(8,128)(2,1)}, bf16[7,28,512]{2,1,0:T(8,128)(2,1)}) custom-call(bf16[7,28,512]{2,1,0:T(8,128)(2,1)} %x_ref.1, bf16[7,28,512]{2,1,0:T(8,128)(2,1)} %cot_ref.1, f32[1,512]{1,0:T(1,128)} %bitcast.3, f32[9,2048]{1,0:T(8,128)} %dw_ref.1, f32[1,512]{1,0:T(1,128)} %bitcast.4, f32[1,512]{1,0:T(1,128)} %bitcast.5, ...), custom_call_target="tpu_custom_call" | custom-call | tf_op jit(solution)/shard_map/mbconv_attention/pallas_call | solution.py:567
  77.3 1.6 %copy.21 = bf16[7,28,512]{2,1,0:T(8,128)(2,1)} copy(bf16[7,28,512]{2,1,0:T(8,128)(2,1)} %get-tuple-element.4) | data formatting | bytes 401408
  79.0 1.6 %copy.22 = bf16[7,28,512]{2,1,0:T(8,128)(2,1)} copy(bf16[7,28,512]{2,1,0:T(8,128)(2,1)} %get-tuple-element.5) | data formatting | bytes 401408

commit v2 on v1

--- a/solution.py
+++ b/solution.py
@@ -18,7 +18,7 @@
 SW = 32
 NWIN, WPAD = 4, 64
 LEN = 49
-CHUNK = 256
+CHUNK = 1024
 EPSILON = 1e-05
 F32, BF16 = jnp.float32, jnp.bfloat16
 MESH = pl.DeviceIdType.MESH
@@ -117,23 +117,10 @@
     return lax.dot_general(a, b, (((0,), (0,)), ((), ())), preferred_element_type=F32)
 
 
-def tail(u):
-    d = 1.0 + (0.3275911 * 0.5**0.5) * jnp.abs(u)
-    t = pl.reciprocal(d, approx=True)
-    t = t * (2.0 - d * t)
-    gauss = jnp.exp(-0.5 * (u * u))
-    poly = 0.5 * 1.061405429
-    for coefficient in (-1.453152027, 1.421413741, -0.284496736, 0.254829592):
-        poly = poly * t + 0.5 * coefficient
-    return poly * t * gauss, gauss
-
-
-def gelu_of(u, half):
-    return jnp.maximum(u, 0.0) - jnp.abs(u) * half
-
-
-def slope_of(u, half, gauss):
-    return jnp.where(u >= 0.0, 1.0 - half, half) + u * gauss * (0.5 / np.pi) ** 0.5
+def gelu_of(u):
+    share = 0.5 + 0.5 * lax.erf(u * 0.5**0.5)
+    density = jnp.exp2((-0.5 / np.log(2.0)) * (u * u))
+    return u * share, share + (u * (0.5 / np.pi) ** 0.5) * density
 
 
 def standardize(x):
@@ -303,9 +290,9 @@
 
     send_chunks(cot_send, cot_recv, grid_sem.at[0], True)
 
-    def flip(bias, bias_t, h):
+    def flip(bias, h):
         square = jnp.concatenate(
-            [bias[h], jnp.zeros((LEN, 128 - LEN), F32)], axis=1
+            [bias[pl.ds(h, LEN, stride=16), :], jnp.zeros((LEN, 128 - LEN), F32)], axis=1
         )
         square = jnp.concatenate([square, jnp.zeros((WPAD - LEN, 128), F32)], axis=0)
         turned = square.T[0:WPAD]
@@ -315,7 +302,7 @@
     def flip_all(bias, bias_t):
         for g in range(4):
             for h in range(2):
-                pair = [flip(bias, bias_t, 4 * g + 2 * h + n) for n in range(2)]
+                pair = [flip(bias, 4 * g + 2 * h + n) for n in range(2)]
                 bias_t[g, :, 128 * h : 128 * (h + 1)] = jnp.concatenate(pair, axis=1)
 
     l_bb.wait()
@@ -348,16 +335,15 @@
     def mbconv(step, carry):
         at = pl.multiple_of(step * CHUNK, CHUNK)
         u = dot(normed0[...], we[:, pl.ds(at, CHUNK)])
-        half, gauss = tail(u)
-        slope_u[:, pl.ds(at, CHUNK)] = slope_of(u, half, gauss)[64:288]
-        e = gelu_of(u, half).astype(BF16).astype(F32)
+        e, slope = gelu_of(u)
+        slope_u[:, pl.ds(at, CHUNK)] = slope[64:288]
+        e = e.astype(BF16).astype(F32)
         w = taps(at)
         y = [sum(e[SW * a : SW * a + 288] * w[3 * a + b] for a in range(3)) for b in range(3)]
         pre = pltpu.roll(y[0], 1, 0) + y[1] + pltpu.roll(y[2], 287, 0)
-        half, gauss = tail(pre)
-        slope_p[:, pl.ds(at, CHUNK)] = slope_of(pre, half, gauss)
-        branch = gelu_of(pre[32:256], half[32:256]).astype(BF16)
-        update[...] += dot(branch, wp[pl.ds(at, CHUNK), :])
+        branch, slope = gelu_of(pre)
+        slope_p[:, pl.ds(at, CHUNK)] = slope
+        update[...] += dot(branch[32:256].astype(BF16), wp[pl.ds(at, CHUNK), :])
         return carry
 
     lax.fori_loop(0, FF // CHUNK, mbconv, 0)
@@ -392,7 +378,7 @@
                 )
             return carry
 
-        lax.fori_loop(0, NWIN, window, 0)
+        lax.fori_loop(0, NWIN, window, 0, unroll=True)
 
     def attend_back(packed, prob):
         def window(w, carry):
@@ -411,7 +397,7 @@
                     dpk[rows, 512 * n + 128 * g : 512 * n + 128 * (g + 1)] = one.astype(BF16)
             return carry
 
-        lax.fori_loop(0, NWIN, window, 0)
+        lax.fori_loop(0, NWIN, window, 0, unroll=True)
 
     def project_back(qkv, gain_ref, xhat_ref, scale_ref):
         dn = dot_nt(dpk[...], qkv[...]).astype(BF16).astype(F32)
@@ -537,11 +523,14 @@
     inputs, cotangent, conv_gain, expand_weight, depth_weight, project_weight,
     block_gain, block_qkv, block_out, block_bias, grid_gain, grid_qkv, grid_out, grid_bias,
 ):
+    def by_query(bias):
+        return bias.transpose(1, 0, 2).reshape(16 * LEN, LEN)
+
     vmem, hbm = pl.BlockSpec(memory_space=pltpu.VMEM), pl.BlockSpec(memory_space=pl.ANY)
     places = jnp.asarray(PLACES, BF16)
     chunks = pltpu.VMEM((LEN, 16, 128), BF16)
     tokens = jax.ShapeDtypeStruct((TR, TC, D), BF16)
-    bias = pltpu.VMEM((16, LEN, LEN), F32)
+    bias = pltpu.VMEM((16 * LEN, LEN), F32)
     bias_t = pltpu.VMEM((4, WPAD, 256), F32)
     win_f32, win_bf16 = pltpu.VMEM((256, D), F32), pltpu.VMEM((256, D), BF16)
     packed = pltpu.VMEM((256, 3 * D), BF16)
@@ -577,7 +566,7 @@
     )(
         inputs, cotangent, conv_gain.reshape(1, D), depth_weight, block_gain.reshape(1, D),
         grid_gain.reshape(1, D), places, expand_weight, project_weight, block_qkv, block_out,
-        block_bias, grid_qkv, grid_out, grid_bias,
+        by_query(block_bias), grid_qkv, grid_out, by_query(grid_bias),
     )
 
 

time: 80.9 us -> 63.3 us (0.78)
  Pallas kernels: 72.9 us -> 59.2 us
  local copies, waits for them, and re-layouts: 7.1 us -> 3.28 us
    pallas_call x1, Pallas kernels: 72.9 us -> 59.2 us  [local(): pl.pallas_call(kernel, out_shape=(tokens, tokens), in_specs=[vmem] * 6 +...]
    unnamed x4 -> x2, local copies, waits for them, and re-layouts: 7.1 us -> 3.28 us
where the time goes in v2:
time: 63.3 us; the launch traced here: 63.1 us
  Pallas kernels  59.2 us (94%)
  local copies, waits for them, and re-layouts  3.28 us (5%)
  between operations  0.64 us (1%)
    pallas_call x1, Pallas kernels, local(): pl.pallas_call(kernel, out_shape=(tokens, tokens), in_specs=[vmem] * 6 +...  59.2 us
    unnamed x2, local copies, waits for them, and re-layouts  3.28 us

profile of v2, /device:TPU:0, one launch (start us, length us, event | category | flops | bytes accessed | tf_op | source)
XLA Modules:
  0.0 63.1 jit_solution(18062498362490735237)
XLA Ops:
  0.6 59.2 %mbconv_attention.1 = (bf16[7,28,512]{2,1,0:T(8,128)(2,1)}, bf16[7,28,512]{2,1,0:T(8,128)(2,1)}) custom-call(bf16[7,28,512]{2,1,0:T(8,128)(2,1)} %x_ref.1, bf16[7,28,512]{2,1,0:T(8,128)(2,1)} %cot_ref.1, f32[1,512]{1,0:T(1,128)} %bitcast.11, f32[9,2048]{1,0:T(8,128)} %dw_ref.1, f32[1,512]{1,0:T(1,128)} %bitcast.12, f32[1,512]{1,0:T(1,128)} %bitcast.13, ...), custom_call_target="tpu_custom_call" | custom-call | tf_op jit(solution)/shard_map/mbconv_attention/pallas_call | solution.py:556
  59.8 1.6 %copy.19 = bf16[7,28,512]{2,1,0:T(8,128)(2,1)} copy(bf16[7,28,512]{2,1,0:T(8,128)(2,1)} %get-tuple-element.4) | data formatting | bytes 401408
  61.4 1.6 %copy.20 = bf16[7,28,512]{2,1,0:T(8,128)(2,1)} copy(bf16[7,28,512]{2,1,0:T(8,128)(2,1)} %get-tuple-element.5) | data formatting | bytes 401408

commit v3 on v2

--- a/solution.py
+++ b/solution.py
@@ -19,6 +19,7 @@
 NWIN, WPAD = 4, 64
 LEN = 49
 CHUNK = 1024
+TILES = CHUNK // 128
 EPSILON = 1e-05
 F32, BF16 = jnp.float32, jnp.bfloat16
 MESH = pl.DeviceIdType.MESH
@@ -29,71 +30,51 @@
 
 
 def placements():
-    halo = np.zeros((352, 448))
-    for rho in range(11):
-        for kappa in range(32):
-            r, c = rho - 2, kappa - 2
-            if 0 <= r < 7:
-                if 0 <= c < 28:
-                    at = 32 * r + c
-                elif c < 0:
-                    at = 352 + 2 * r + c + 2
-                else:
-                    at = 368 + 2 * r + c - 28
-            elif r < 0:
-                if 0 <= c < 28:
-                    at = 224 + 32 * (r + 2) + c
-                elif c < 0:
-                    at = 384 + 2 * (r + 7) + c + 2
-                else:
-                    at = 400 + 2 * (r + 7) + c - 28
-            else:
-                if 0 <= c < 28:
-                    at = 288 + 32 * (r - 7) + c
-                elif c < 0:
-                    at = 416 + 2 * (r - 7) + c + 2
-                else:
-                    at = 432 + 2 * (r - 7) + c - 28
-            halo[32 * rho + kappa, at] = 1
-    edge = np.zeros((32, 448))
-    for r in range(7):
+    edge = np.zeros((32, 256))
+    slots = np.zeros((256, 256))
+    to_win = np.zeros((256, 256))
+    from_win = np.zeros((208, 256))
+    back_win = np.zeros((256, 256))
+    for r in range(TR):
         for c in range(2):
-            edge[2 * r + c, 32 * r + c] = 1
-            edge[16 + 2 * r + c, 32 * r + 26 + c] = 1
-    to_win = np.zeros((256, 448))
-    from_win = np.zeros((208, 448))
-    back_win = np.zeros((256, 448))
-    for r in range(7):
-        for c in range(28):
-            to_win[win_row(r, c), 32 * r + c + 2] = 1
-            from_win[28 * r + c, win_row(r, c)] = 1
-            back_win[win_row(r, c), 28 * r + c] = 1
-    edge2 = np.zeros((96, 448))
-    for c in range(28):
-        edge2[c, win_row(0, c)] = 1
-        edge2[32 + c, win_row(6, c)] = 1
-    for r in range(7):
-        edge2[64 + r, win_row(r, 0)] = 1
-        edge2[80 + r, win_row(r, 27)] = 1
-    halo2 = np.zeros((288, 448))
-    for rho in range(9):
-        for kappa in range(1, 31):
-            r, c = rho - 1, kappa - 2
-            if 0 <= r < 7:
-                if 0 <= c < 28:
-                    at = win_row(r, c)
-                elif c < 0:
-                    at = 320 + r
-                else:
-                    at = 336 + r
-            elif r < 0:
-                at = 256 + c if 0 <= c < 28 else (352 + 6 if c < 0 else 368 + 6)
-            else:
-                at = 288 + c if 0 <= c < 28 else (384 if c < 0 else 400)
-            halo2[32 * rho + kappa, at] = 1
+            edge[2 * r + c, SW * r + c + 2] = 1
+            edge[16 + 2 * r + c, SW * r + c + 28] = 1
+        for c in range(TC):
+            to_win[win_row(r, c), SW * r + c + 2] = 1
+            slots[SW * r + c + 2, win_row(r, c)] = 1
+            from_win[TC * r + c, win_row(r, c)] = 1
+            back_win[win_row(r, c), TC * r + c] = 1
+        slots[224 + r, win_row(r, 0)] = 1
+        slots[240 + r, win_row(r, 27)] = 1
+    halo = np.zeros((192, 256))
+    for line in range(2):
+        for c in range(TC):
+            for half in range(2):
+                at = 64 * half + SW * line + c + 2
+                halo[at, at] = 1
+        for c in range(2):
+            for half in range(2):
+                for side in range(2):
+                    at = 64 * half + SW * line + (30 * side + c)
+                    row = line + (0 if half else 5)
+                    halo[at, 128 + 16 * (2 + 2 * half + side) + 2 * row + c] = 1
+    for r in range(TR):
+        for c in range(2):
+            for side in range(2):
+                halo[128 + 16 * (2 * side + c) + r + 2, 128 + 16 * side + 2 * r + c] = 1
+    halo2 = np.zeros((96, 256))
+    for half in range(2):
+        for c in range(TC):
+            halo2[32 * half + c + 2, 32 * half + c + 2] = 1
+        for side in range(2):
+            row = 0 if half else 6
+            halo2[32 * half + 1 + 29 * side, 64 + 16 * (2 + 2 * half + side) + row] = 1
+    for r in range(TR):
+        for side in range(2):
+            halo2[64 + 16 * side + r, 64 + 16 * side + r] = 1
     parts = dict(
-        halo=halo, edge=edge, to_win=to_win, from_win=from_win, back_win=back_win,
-        edge2=edge2, halo2=halo2,
+        edge=edge, halo=halo, to_win=to_win, from_win=from_win, back_win=back_win,
+        slots=slots, halo2=halo2,
     )
     starts, at = {}, 0
     for name, part in parts.items():
@@ -156,11 +137,11 @@
     places_hbm, we_hbm, wp_hbm, bqkv_hbm, bout_hbm, bbias_hbm, gqkv_hbm, gout_hbm, gbias_hbm,
     out_ref, grad_ref,
     places, we, wp, bqkv, bout, bbias, gqkv, gout, gbias, load_sem,
-    stage, cat, edges, cat2, edges2, halo_sem, halo2_sem,
+    stage, own, cat, edges, own2, cat2, halo_sem, halo2_sem,
     cot_send, cot_recv, fwd_send, fwd_recv, res_send, res_recv, gra_send, gra_recv, grid_sem,
-    mixbuf, xhat0, scale0, normed0, slope_u, slope_p, update,
+    mixbuf, xhat0, scale0, normed0, normed1, slope_u, slope_p, pre_act, update,
     bias_b, bias_g, zwin, packed_b, xhat_b, scale_b, prob_b, att,
-    zgrid, dgrid, packed_g, xhat_g, scale_g, prob_g, dout, da, dpk, gslot,
+    zgrid, dgrid, packed_g, xhat_g, scale_g, prob_g, dout, da, dpk, halo_grad, grad_e,
 ):
     i, j = lax.axis_index("rows"), lax.axis_index("cols")
     me = i * COLS + j
@@ -200,10 +181,10 @@
 
     stage[...] = jnp.zeros_like(stage)
     for r in range(TR):
-        stage[SW * r : SW * r + TC, :] = x_ref[r].astype(F32)
-    cat[0:224, :] = stage[0:224, :].astype(BF16)
+        stage[SW * r + 2 : SW * r + 2 + TC, :] = x_ref[r].astype(F32)
+    own[...] = stage[...].astype(BF16)
     l_places.wait()
-    edges[...] = place("edge", cat[0:224, :]).astype(BF16)
+    edges[...] = place("edge", own[...]).astype(BF16)
 
     mixbuf[...] = jnp.zeros_like(mixbuf)
     for r in range(TR):
@@ -213,6 +194,78 @@
             ].astype(F32)
     cot_send[...] = mixbuf[0:784, :].reshape(LEN, 16, 128).astype(BF16)
 
+    def flip(bias, h):
+        square = jnp.concatenate(
+            [bias[pl.ds(h, LEN, stride=16), :], jnp.zeros((LEN, 128 - LEN), F32)], axis=1
+        )
+        square = jnp.concatenate([square, jnp.zeros((WPAD - LEN, 128), F32)], axis=0)
+        turned = square.T[0:WPAD]
+        key = lax.broadcasted_iota(jnp.int32, (WPAD, WPAD), 0)
+        return jnp.where(key < LEN, turned, -1e30)
+
+    def flip_all(bias, bias_t):
+        for g in range(4):
+            for h in range(2):
+                pair = [flip(bias, 4 * g + 2 * h + n) for n in range(2)]
+                bias_t[g, :, 128 * h : 128 * (h + 1)] = jnp.concatenate(pair, axis=1)
+
+    l_bb.wait()
+    flip_all(bbias, bias_b)
+    l_gb.wait()
+    flip_all(gbias, bias_g)
+
+    xhat, scale = standardize(stage[...])
+    xhat0[...] = xhat
+    scale0[...] = scale
+    normed0[...] = (xhat * cgain_ref[...]).astype(BF16)
+    l_we.wait()
+
+    def taps(at):
+        return [dw_ref[n : n + 1, pl.ds(at, CHUNK)] for n in range(9)]
+
+    def wide(ref, step, rows=slice(None)):
+        return jnp.concatenate([ref[step * TILES + n, rows, :] for n in range(TILES)], axis=1)
+
+    def put_wide(ref, step, rows, value):
+        for n in range(TILES):
+            ref[step * TILES + n, rows, :] = value[:, 128 * n : 128 * (n + 1)]
+
+    def add_wide(ref, step, first, value):
+        rows = slice(first, first + value.shape[0])
+        put_wide(ref, step, rows, wide(ref, step, rows) + value)
+
+    def lines(x, first, last):
+        return x[SW * first : SW * last]
+
+    def side_by_side(y):
+        count = y[0].shape[0]
+        return pltpu.roll(y[0], 1, 0) + y[1] + pltpu.roll(y[2], count - 1, 0)
+
+    def expand_own(step, carry):
+        at = pl.multiple_of(step * CHUNK, CHUNK)
+        e, slope = gelu_of(dot(normed0[...], we[:, pl.ds(at, CHUNK)]))
+        slope_u[:, pl.ds(at, CHUNK)] = slope
+        e = e.astype(BF16).astype(F32)
+        w = taps(at)
+        y = []
+        for b in range(3):
+            t = [e * w[3 * a + b] for a in range(3)]
+            y.append(
+                jnp.concatenate(
+                    [
+                        lines(t[2], 0, 1),
+                        lines(t[1], 0, 1) + lines(t[2], 1, 2),
+                        lines(t[0], 0, 5) + lines(t[1], 1, 6) + lines(t[2], 2, 7),
+                        lines(t[0], 5, 6) + lines(t[1], 6, 7),
+                        lines(t[0], 6, 7),
+                    ],
+                    axis=0,
+                )
+            )
+        put_wide(pre_act, step, slice(None), side_by_side(y))
+        return carry
+
+    lax.fori_loop(0, 1, expand_own, 0)
     pl.semaphore_wait(barrier, ROWS * COLS - 1)
 
     north, south = lax.rem(i + ROWS - 1, ROWS), lax.rem(i + 1, ROWS)
@@ -234,14 +287,14 @@
     halo = swap(
         halo_sem,
         [
-            (cat.at[pl.ds(0, 64)], cat.at[pl.ds(288, 64)], (north, j)),
-            (cat.at[pl.ds(160, 64)], cat.at[pl.ds(224, 64)], (south, j)),
-            (e_cols, cat.at[pl.ds(352, 16)], (i, east)),
-            (w_cols, cat.at[pl.ds(368, 16)], (i, west)),
-            (e_cols, cat.at[pl.ds(384, 16)], (south, east)),
-            (w_cols, cat.at[pl.ds(400, 16)], (south, west)),
-            (e_cols, cat.at[pl.ds(416, 16)], (north, east)),
-            (w_cols, cat.at[pl.ds(432, 16)], (north, west)),
+            (own.at[pl.ds(0, 64)], cat.at[pl.ds(64, 64)], (north, j)),
+            (own.at[pl.ds(160, 64)], cat.at[pl.ds(0, 64)], (south, j)),
+            (e_cols, cat.at[pl.ds(128, 16)], (i, east)),
+            (w_cols, cat.at[pl.ds(144, 16)], (i, west)),
+            (e_cols, cat.at[pl.ds(160, 16)], (south, east)),
+            (w_cols, cat.at[pl.ds(176, 16)], (south, west)),
+            (e_cols, cat.at[pl.ds(192, 16)], (north, east)),
+            (w_cols, cat.at[pl.ds(208, 16)], (north, west)),
         ],
     )
 
@@ -290,64 +343,66 @@
 
     send_chunks(cot_send, cot_recv, grid_sem.at[0], True)
 
-    def flip(bias, h):
-        square = jnp.concatenate(
-            [bias[pl.ds(h, LEN, stride=16), :], jnp.zeros((LEN, 128 - LEN), F32)], axis=1
-        )
-        square = jnp.concatenate([square, jnp.zeros((WPAD - LEN, 128), F32)], axis=0)
-        turned = square.T[0:WPAD]
-        key = lax.broadcasted_iota(jnp.int32, (WPAD, WPAD), 0)
-        return jnp.where(key < LEN, turned, -1e30)
-
-    def flip_all(bias, bias_t):
-        for g in range(4):
-            for h in range(2):
-                pair = [flip(bias, 4 * g + 2 * h + n) for n in range(2)]
-                bias_t[g, :, 128 * h : 128 * (h + 1)] = jnp.concatenate(pair, axis=1)
-
-    l_bb.wait()
-    flip_all(bbias, bias_b)
-    l_gb.wait()
-    flip_all(gbias, bias_g)
+    lax.fori_loop(1, FF // CHUNK, expand_own, 0)
 
     for one in halo:
         one.wait_recv()
-
-    def inside(count, row_shift):
-        slot = lax.broadcasted_iota(jnp.int32, (count, 1), 0)
-        row = TR * i + lax.shift_right_logical(slot, 5) - row_shift
-        col = TC * j + lax.bitwise_and(slot, 31) - 2
-        return (row >= 0) & (row < HEIGHT) & (col >= 0) & (col < BREADTH)
-
-    xh = jnp.where(inside(352, 2), place("halo", cat[...]), 0.0)
-    xhat, scale = standardize(xh)
-    xhat0[...] = xhat[64:288]
-    scale0[...] = scale[64:288]
-    stage[0:224, :] = xh[64:288]
-    normed0[...] = (xhat * cgain_ref[...]).astype(BF16)
+    has_n, has_s, has_w, has_e = (
+        jnp.where(there, 1.0, 0.0) for there in (i > 0, i < ROWS - 1, j > 0, j < COLS - 1)
+    )
+
+    def inside(count, strip, column):
+        at = lax.broadcasted_iota(jnp.int32, (count, 1), 0)
+        slot = lax.bitwise_and(at, SW - 1)
+        keep = jnp.where(slot < 2, has_w, 1.0) * jnp.where(slot < 30, 1.0, has_e)
+        strips = jnp.where(at < strip, has_n, has_s) * keep
+        columns = jnp.where(at < 2 * strip + column, has_w, has_e)
+        return jnp.where(at < 2 * strip, strips, columns)
+
+    xh = place("halo", cat[...]) * inside(192, 64, 32)
+    normed1[...] = (standardize(xh)[0] * cgain_ref[...]).astype(BF16)
     update[...] = jnp.zeros_like(update)
-    l_we.wait()
     l_wp.wait()
 
-    def taps(at):
-        return [dw_ref[n : n + 1, pl.ds(at, CHUNK)] for n in range(9)]
+    def add_column(ref, slot, count, step, value):
+        rows = pl.ds(slot, count, stride=SW)
+        put_wide(ref, step, rows, wide(ref, step, rows) + value[0:count])
 
     def mbconv(step, carry):
         at = pl.multiple_of(step * CHUNK, CHUNK)
-        u = dot(normed0[...], we[:, pl.ds(at, CHUNK)])
-        e, slope = gelu_of(u)
-        slope_u[:, pl.ds(at, CHUNK)] = slope[64:288]
+        here = pl.ds(at, CHUNK)
+        e, _ = gelu_of(dot(normed1[...], we[:, here]))
         e = e.astype(BF16).astype(F32)
         w = taps(at)
-        y = [sum(e[SW * a : SW * a + 288] * w[3 * a + b] for a in range(3)) for b in range(3)]
-        pre = pltpu.roll(y[0], 1, 0) + y[1] + pltpu.roll(y[2], 287, 0)
-        branch, slope = gelu_of(pre)
-        slope_p[:, pl.ds(at, CHUNK)] = slope
-        update[...] += dot(branch[32:256].astype(BF16), wp[pl.ds(at, CHUNK), :])
+        n0, n1, s0, s1 = (lines(e, n, n + 1) for n in range(4))
+        w0, w1, e0, e1 = (e[128 + 16 * n : 144 + 16 * n] for n in range(4))
+        around = [
+            (0, [n0 * w[b] + n1 * w[3 + b] for b in range(3)]),
+            (32, [n1 * w[b] for b in range(3)]),
+            (224, [s0 * w[6 + b] for b in range(3)]),
+            (256, [s0 * w[3 + b] + s1 * w[6 + b] for b in range(3)]),
+        ]
+        for first, y in around:
+            add_wide(pre_act, step, first, side_by_side(y))
+
+        def down(terms):
+            return terms[0] + pltpu.roll(terms[1], 15, 0) + pltpu.roll(terms[2], 14, 0)
+
+        sides = [
+            (1, [w0 * w[3 * a] + w1 * w[3 * a + 1] for a in range(3)]),
+            (2, [w1 * w[3 * a] for a in range(3)]),
+            (29, [e0 * w[3 * a + 2] for a in range(3)]),
+            (30, [e0 * w[3 * a + 1] + e1 * w[3 * a + 2] for a in range(3)]),
+        ]
+        for slot, terms in sides:
+            add_column(pre_act, slot, 9, step, down(terms))
+        branch, slope = gelu_of(wide(pre_act, step))
+        put_wide(slope_p, step, slice(None), slope)
+        update[...] += dot(branch[32:256].astype(BF16), wp[here, :])
         return carry
 
     lax.fori_loop(0, FF // CHUNK, mbconv, 0)
-    mixed = (stage[0:224, :] + update[...]).astype(BF16)
+    mixed = (stage[...] + update[...]).astype(BF16)
     zwin[...] = place("to_win", mixed)
 
     root = HEAD_DIM**-0.5
@@ -460,63 +515,100 @@
     dout[...] = place("back_win", spatial.astype(BF16)).astype(BF16)
     da[...] = dot_nt(dout[...], bout[...]).astype(BF16)
     attend_back(packed_b, prob_b)
-    cat2[0:256, :] = project_back(bqkv, bgain_ref, xhat_b, scale_b)
-    edges2[...] = place("edge2", cat2[0:256, :]).astype(BF16)
-    w_col2, e_col2 = edges2.at[pl.ds(64, 16)], edges2.at[pl.ds(80, 16)]
+    slotted = place("slots", project_back(bqkv, bgain_ref, xhat_b, scale_b))
+    stage[...] = slotted[0:224]
+    own2[...] = slotted.astype(BF16)
+    w_col2, e_col2 = own2.at[pl.ds(224, 16)], own2.at[pl.ds(240, 16)]
     halo2 = swap(
         halo2_sem,
         [
-            (edges2.at[pl.ds(0, 32)], cat2.at[pl.ds(288, 32)], (north, j)),
-            (edges2.at[pl.ds(32, 32)], cat2.at[pl.ds(256, 32)], (south, j)),
-            (e_col2, cat2.at[pl.ds(320, 16)], (i, east)),
-            (w_col2, cat2.at[pl.ds(336, 16)], (i, west)),
-            (e_col2, cat2.at[pl.ds(352, 16)], (south, east)),
-            (w_col2, cat2.at[pl.ds(368, 16)], (south, west)),
-            (e_col2, cat2.at[pl.ds(384, 16)], (north, east)),
-            (w_col2, cat2.at[pl.ds(400, 16)], (north, west)),
+            (own2.at[pl.ds(0, 32)], cat2.at[pl.ds(32, 32)], (north, j)),
+            (own2.at[pl.ds(192, 32)], cat2.at[pl.ds(0, 32)], (south, j)),
+            (e_col2, cat2.at[pl.ds(64, 16)], (i, east)),
+            (w_col2, cat2.at[pl.ds(80, 16)], (i, west)),
+            (e_col2, cat2.at[pl.ds(96, 16)], (south, east)),
+            (w_col2, cat2.at[pl.ds(112, 16)], (south, west)),
+            (e_col2, cat2.at[pl.ds(128, 16)], (north, east)),
+            (w_col2, cat2.at[pl.ds(144, 16)], (north, west)),
         ],
     )
 
+    def back_own(step, carry):
+        here = pl.ds(pl.multiple_of(step * CHUNK, CHUNK), CHUNK)
+        gp = dot_nt(own2[0:224, :], wp[here, :]).astype(BF16).astype(F32)
+        gp = gp * wide(slope_p, step, slice(32, 256))
+        w = taps(pl.multiple_of(step * CHUNK, CHUNK))
+        y = []
+        for b in range(3):
+            t = [gp * w[3 * a + 2 - b] for a in range(3)]
+            y.append(
+                jnp.concatenate(
+                    [
+                        lines(t[0], 1, 2) + lines(t[1], 0, 1),
+                        lines(t[0], 2, 7) + lines(t[1], 1, 6) + lines(t[2], 0, 5),
+                        lines(t[1], 6, 7) + lines(t[2], 5, 6),
+                    ],
+                    axis=0,
+                )
+            )
+        put_wide(grad_e, step, slice(None), side_by_side(y))
+        return carry
+
+    lax.fori_loop(0, FF // CHUNK, back_own, 0)
+    update[...] = jnp.zeros_like(update)
     wait_chunks(res_recv, grid_sem.at[2])
-    mixbuf[0:784, :] = res_recv[...].astype(F32).reshape(784, 128)
+    out_ref[...] = res_recv[...]
+
+    for one in halo2:
+        one.wait_recv()
+    gm = place("halo2", cat2[...]) * inside(96, 32, 16)
+    halo_grad[...] = gm.astype(BF16)
+
+    def mbconv_back(step, carry):
+        at = pl.multiple_of(step * CHUNK, CHUNK)
+        here = pl.ds(at, CHUNK)
+        gp = dot_nt(halo_grad[...], wp[here, :]).astype(BF16).astype(F32)
+        w = taps(at)
+
+        north_gp = gp[0:32] * wide(slope_p, step, slice(0, 32))
+        south_gp = gp[32:64] * wide(slope_p, step, slice(256, 288))
+        west_gp = gp[64:72] * wide(slope_p, step, pl.ds(SW + 1, 8, stride=SW))
+        east_gp = gp[80:88] * wide(slope_p, step, pl.ds(SW + 30, 8, stride=SW))
+        add_wide(grad_e, step, 0, side_by_side([north_gp * w[8 - b] for b in range(3)]))
+        add_wide(grad_e, step, 192, side_by_side([south_gp * w[2 - b] for b in range(3)]))
+
+        def down(x, b):
+            return (
+                pltpu.roll(x * w[b], 7, 0) + x * w[3 + b] + pltpu.roll(x * w[6 + b], 1, 0)
+            )
+
+        add_column(grad_e, 2, 7, step, down(west_gp, 2))
+        add_column(grad_e, 29, 7, step, down(east_gp, 0))
+        gh = wide(grad_e, step).astype(BF16).astype(F32) * slope_u[:, here]
+        update[...] += dot_nt(gh.astype(BF16), we[:, here])
+        return carry
+
+    lax.fori_loop(0, FF // CHUNK, mbconv_back, 0)
+    dn = update[...].astype(BF16).astype(F32)
+    dx = standardize_back(dn * cgain_ref[...], xhat0[...], scale0[...])
+    stage[...] = stage[...] + dx.astype(BF16).astype(F32)
+    for r in range(TR):
+        grad_ref[r] = stage[SW * r + 2 : SW * r + 2 + TC, :].astype(BF16)
+
+    for one in halo + halo2:
+        one.wait_send()
+    for n, send in enumerate((cot_send, fwd_send, res_send, gra_send)):
+        wait_sent(send, grid_sem.at[n])
+
+
+def finish(chunks_ref, kept_ref, out_ref, grad_ref, mixbuf):
+    mixbuf[...] = chunks_ref[...].astype(F32).reshape(784, 128)
     for r in range(TR):
         for k in range(4):
             out_ref[r, :, 128 * k : 128 * (k + 1)] = mixbuf[
                 pl.ds(112 * r + k, TC, stride=4), :
             ].astype(BF16)
-
-    for one in halo2:
-        one.wait_recv()
-    gm = jnp.where(inside(288, 1), place("halo2", cat2[...]), 0.0)
-    stage[0:224, :] = gm[32:256]
-    gslot[...] = gm.astype(BF16)
-    update[...] = jnp.zeros_like(update)
-
-    def mbconv_back(step, carry):
-        at = pl.multiple_of(step * CHUNK, CHUNK)
-        gp = dot_nt(gslot[...], wp[pl.ds(at, CHUNK), :]).astype(BF16).astype(F32)
-        gp = gp * slope_p[:, pl.ds(at, CHUNK)]
-        w = taps(at)
-        y = [
-            sum(gp[SW * (2 - a) : SW * (2 - a) + 224] * w[3 * a + b] for a in range(3))
-            for b in range(3)
-        ]
-        ge = pltpu.roll(y[0], 223, 0) + y[1] + pltpu.roll(y[2], 1, 0)
-        gh = ge.astype(BF16).astype(F32) * slope_u[:, pl.ds(at, CHUNK)]
-        update[...] += dot_nt(gh.astype(BF16), we[:, pl.ds(at, CHUNK)])
-        return carry
-
-    lax.fori_loop(0, FF // CHUNK, mbconv_back, 0)
-    dn = update[...].astype(BF16).astype(F32)
-    dx = standardize_back(dn * cgain_ref[...], xhat0[...], scale0[...])
-    stage[0:224, :] = stage[0:224, :] + dx.astype(BF16).astype(F32)
-    for r in range(TR):
-        grad_ref[r] = stage[SW * r + 2 : SW * r + 2 + TC, :].astype(BF16)
-
-    for one in halo + halo2:
-        one.wait_send()
-    for n, send in enumerate((cot_send, fwd_send, res_send, gra_send)):
-        wait_sent(send, grid_sem.at[n])
+    grad_ref[...] = kept_ref[...]
 
 
 def local(
@@ -541,21 +633,22 @@
         pltpu.VMEM((D, 3 * D), BF16), pltpu.VMEM((D, D), BF16), bias,
         pltpu.VMEM((D, 3 * D), BF16), pltpu.VMEM((D, D), BF16), bias,
         pltpu.SemaphoreType.DMA((9,)),
-        pltpu.VMEM((224, D), F32), pltpu.VMEM((448, D), BF16), pltpu.VMEM((32, D), BF16),
-        pltpu.VMEM((416, D), BF16), pltpu.VMEM((96, D), BF16),
+        pltpu.VMEM((224, D), F32), pltpu.VMEM((224, D), BF16), pltpu.VMEM((224, D), BF16),
+        pltpu.VMEM((32, D), BF16), pltpu.VMEM((256, D), BF16), pltpu.VMEM((160, D), BF16),
         pltpu.SemaphoreType.DMA((2, 8)), pltpu.SemaphoreType.DMA((2, 8)),
         chunks, chunks, chunks, chunks, chunks, chunks, chunks, chunks,
         pltpu.SemaphoreType.DMA((4, 2)),
         pltpu.VMEM((832, 128), F32), pltpu.VMEM((224, D), F32), pltpu.VMEM((224, 1), F32),
-        pltpu.VMEM((352, D), BF16), pltpu.VMEM((224, FF), F32), pltpu.VMEM((288, FF), F32),
+        pltpu.VMEM((224, D), BF16), pltpu.VMEM((192, D), BF16), pltpu.VMEM((224, FF), F32),
+        pltpu.VMEM((FF // 128, 288, 128), F32), pltpu.VMEM((FF // 128, 288, 128), F32),
         pltpu.VMEM((224, D), F32),
         bias_t, bias_t, win_f32, packed, win_f32, scale, prob, win_bf16,
         win_f32, win_f32, packed, win_f32, scale, prob, win_bf16, win_bf16, packed,
-        pltpu.VMEM((288, D), BF16),
+        pltpu.VMEM((96, D), BF16), pltpu.VMEM((FF // 128, 224, 128), F32),
     ]
-    return pl.pallas_call(
+    result, grad = pl.pallas_call(
         kernel,
-        out_shape=(tokens, tokens),
+        out_shape=(jax.ShapeDtypeStruct((LEN, 16, 128), BF16), tokens),
         in_specs=[vmem] * 6 + [hbm] * 9,
         out_specs=(vmem, vmem),
         scratch_shapes=scratch,
@@ -568,6 +661,14 @@
         grid_gain.reshape(1, D), places, expand_weight, project_weight, block_qkv, block_out,
         by_query(block_bias), grid_qkv, grid_out, by_query(grid_bias),
     )
+    return pl.pallas_call(
+        finish,
+        out_shape=(tokens, tokens),
+        in_specs=[vmem] * 2,
+        out_specs=(vmem, vmem),
+        scratch_shapes=[pltpu.VMEM((784, 128), F32)],
+        name="finish",
+    )(result, grad)
 
 
 def solution(mesh):

time: 63.3 us -> 59.5 us (0.940)
  local copies, waits for them, and re-layouts: 3.28 us -> 0 us
    unnamed x2 -> x0, local copies, waits for them, and re-layouts: 3.28 us -> none
    pallas_call x1 -> x2, Pallas kernels: 59.2 us -> 58.7 us  [the longest x1 56.8 us: local(): pl.pallas_call(kernel, out_shape=(jax.ShapeDtypeStruct((LEN, 16, 128), BF...]
where the time goes in v3:
time: 59.5 us; the launch traced here: 59.3 us
  Pallas kernels  58.7 us (99%)
  between operations  0.64 us (1%)
    pallas_call x1, Pallas kernels, local(): pl.pallas_call(kernel, out_shape=(jax.ShapeDtypeStruct((LEN, 16, 128), BF...  56.8 us
    pallas_call x1, Pallas kernels, local(): pl.pallas_call(finish, out_shape=(tokens, tokens), in_specs=[vmem] * 2, o...  1.87 us

profile of v3, /device:TPU:0, one launch (start us, length us, event | category | flops | bytes accessed | tf_op | source)
XLA Modules:
  0.0 59.3 jit_solution(15977746020729348662)
XLA Ops:
  0.6 56.8 %mbconv_attention.1 = (bf16[49,16,128]{2,1,0:T(8,128)(2,1)}, bf16[7,28,512]{2,1,0:T(8,128)(2,1)}) custom-call(bf16[7,28,512]{2,1,0:T(8,128)(2,1)} %x_ref.1, bf16[7,28,512]{2,1,0:T(8,128)(2,1)} %cot_ref.1, f32[1,512]{1,0:T(1,128)} %bitcast.11, f32[9,2048]{1,0:T(8,128)} %dw_ref.1, f32[1,512]{1,0:T(1,128)} %bitcast.12, f32[1,512]{1,0:T(1,128)} %bitcast.13, ...), custom_call_target="tpu_custom_call" | custom-call | tf_op jit(solution)/shard_map/mbconv_attention/pallas_call | solution.py:649
  57.5 1.9 %finish.1 = (bf16[7,28,512]{2,1,0:T(8,128)(2,1)}, bf16[7,28,512]{2,1,0:T(8,128)(2,1)}) custom-call(bf16[49,16,128]{2,1,0:T(8,128)(2,1)} %get-tuple-element.4.chunks_ref, bf16[7,28,512]{2,1,0:T(8,128)(2,1)} %get-tuple-element.5.kept_ref), custom_call_target="tpu_custom_call" | custom-call | tf_op jit(solution)/shard_map/finish/pallas_call | solution.py:664

commit v4 on v3

--- a/solution.py
+++ b/solution.py
@@ -18,7 +18,7 @@
 SW = 32
 NWIN, WPAD = 4, 64
 LEN = 49
-CHUNK = 1024
+CHUNK = 2048
 TILES = CHUNK // 128
 EPSILON = 1e-05
 F32, BF16 = jnp.float32, jnp.bfloat16
@@ -141,7 +141,7 @@
     cot_send, cot_recv, fwd_send, fwd_recv, res_send, res_recv, gra_send, gra_recv, grid_sem,
     mixbuf, xhat0, scale0, normed0, normed1, slope_u, slope_p, pre_act, update,
     bias_b, bias_g, zwin, packed_b, xhat_b, scale_b, prob_b, att,
-    zgrid, dgrid, packed_g, xhat_g, scale_g, prob_g, dout, da, dpk, halo_grad, grad_e,
+    zgrid, dgrid, packed_g, xhat_g, scale_g, prob_g, dout, da, dpk, dscore, halo_grad, grad_e,
 ):
     i, j = lax.axis_index("rows"), lax.axis_index("cols")
     me = i * COLS + j
@@ -426,14 +426,20 @@
                 q, k, v = parts_of(packed, rows, g)
                 s = dot_nt(k, by_head(q)) * root + bias_t[g]
                 e = jnp.exp(s - jnp.max(s, axis=0, keepdims=True))
-                p = e * (1.0 / jnp.sum(e, axis=0, keepdims=True))
-                prob[w, g] = p
-                att[rows, 128 * g : 128 * (g + 1)] = own_head(dot_tn(p.astype(BF16), v)).astype(
-                    BF16
-                )
+                prob[w, g] = e * (1.0 / jnp.sum(e, axis=0, keepdims=True))
             return carry
 
         lax.fori_loop(0, NWIN, window, 0, unroll=True)
+
+        def gather(w, carry):
+            rows = pl.ds(pl.multiple_of(w * WPAD, WPAD), WPAD)
+            for g in range(4):
+                v = parts_of(packed, rows, g)[2]
+                one = own_head(dot_tn(prob[w, g].astype(BF16), v))
+                att[rows, 128 * g : 128 * (g + 1)] = one.astype(BF16)
+            return carry
+
+        lax.fori_loop(0, NWIN, gather, 0, unroll=True)
 
     def attend_back(packed, prob):
         def window(w, carry):
@@ -445,14 +451,24 @@
                 dp = dot_nt(v, dam).astype(BF16).astype(F32)
                 ds = p * (dp - jnp.sum(p * dp, axis=0, keepdims=True))
                 ds = ds.astype(BF16)
-                dq = own_head(dot_tn(ds, k)) * root
+                dscore[w, g] = ds
                 dk = dot(ds, by_head(q)) * root
                 dv = dot(p.astype(BF16), dam)
-                for n, one in enumerate((dq, dk, dv)):
+                for n, one in ((1, dk), (2, dv)):
                     dpk[rows, 512 * n + 128 * g : 512 * n + 128 * (g + 1)] = one.astype(BF16)
             return carry
 
         lax.fori_loop(0, NWIN, window, 0, unroll=True)
+
+        def queries(w, carry):
+            rows = pl.ds(pl.multiple_of(w * WPAD, WPAD), WPAD)
+            for g in range(4):
+                k = parts_of(packed, rows, g)[1]
+                dq = own_head(dot_tn(dscore[w, g], k)) * root
+                dpk[rows, 128 * g : 128 * (g + 1)] = dq.astype(BF16)
+            return carry
+
+        lax.fori_loop(0, NWIN, queries, 0, unroll=True)
 
     def project_back(qkv, gain_ref, xhat_ref, scale_ref):
         dn = dot_nt(dpk[...], qkv[...]).astype(BF16).astype(F32)
@@ -644,7 +660,8 @@
         pltpu.VMEM((224, D), F32),
         bias_t, bias_t, win_f32, packed, win_f32, scale, prob, win_bf16,
         win_f32, win_f32, packed, win_f32, scale, prob, win_bf16, win_bf16, packed,
-        pltpu.VMEM((96, D), BF16), pltpu.VMEM((FF // 128, 224, 128), F32),
+        pltpu.VMEM((NWIN, 4, WPAD, 256), BF16), pltpu.VMEM((96, D), BF16),
+        pltpu.VMEM((FF // 128, 224, 128), F32),
     ]
     result, grad = pl.pallas_call(
         kernel,

time: 59.5 us -> 53.5 us (0.90)
  Pallas kernels: 58.7 us -> 52.7 us
    pallas_call x1, Pallas kernels: 56.8 us -> 50.8 us  [local(): pl.pallas_call(kernel, out_shape=(jax.ShapeDtypeStruct((LEN, 16, 128), BF...]
where the time goes in v4:
time: 53.5 us; the launch traced here: 53.3 us
  Pallas kernels  52.7 us (99%)
  between operations  0.64 us (1%)
    pallas_call x1, Pallas kernels, local(): pl.pallas_call(kernel, out_shape=(jax.ShapeDtypeStruct((LEN, 16, 128), BF...  50.8 us
    pallas_call x1, Pallas kernels, local(): pl.pallas_call(finish, out_shape=(tokens, tokens), in_specs=[vmem] * 2, o...  1.87 us

profile of v4, /device:TPU:0, one launch (start us, length us, event | category | flops | bytes accessed | tf_op | source)
XLA Modules:
  0.0 53.3 jit_solution(12970688187847962051)
XLA Ops:
  0.6 50.8 %mbconv_attention.1 = (bf16[49,16,128]{2,1,0:T(8,128)(2,1)}, bf16[7,28,512]{2,1,0:T(8,128)(2,1)}) custom-call(bf16[7,28,512]{2,1,0:T(8,128)(2,1)} %x_ref.1, bf16[7,28,512]{2,1,0:T(8,128)(2,1)} %cot_ref.1, f32[1,512]{1,0:T(1,128)} %bitcast.11, f32[9,2048]{1,0:T(8,128)} %dw_ref.1, f32[1,512]{1,0:T(1,128)} %bitcast.12, f32[1,512]{1,0:T(1,128)} %bitcast.13, ...), custom_call_target="tpu_custom_call" | custom-call | tf_op jit(solution)/shard_map/mbconv_attention/pallas_call | solution.py:666
  51.4 1.9 %finish.1 = (bf16[7,28,512]{2,1,0:T(8,128)(2,1)}, bf16[7,28,512]{2,1,0:T(8,128)(2,1)}) custom-call(bf16[49,16,128]{2,1,0:T(8,128)(2,1)} %get-tuple-element.4.chunks_ref, bf16[7,28,512]{2,1,0:T(8,128)(2,1)} %get-tuple-element.5.kept_ref), custom_call_target="tpu_custom_call" | custom-call | tf_op jit(solution)/shard_map/finish/pallas_call | solution.py:681

commit v5 on v4

--- a/solution.py
+++ b/solution.py
@@ -18,8 +18,6 @@
 SW = 32
 NWIN, WPAD = 4, 64
 LEN = 49
-CHUNK = 2048
-TILES = CHUNK // 128
 EPSILON = 1e-05
 F32, BF16 = jnp.float32, jnp.bfloat16
 MESH = pl.DeviceIdType.MESH
@@ -46,7 +44,7 @@
             back_win[win_row(r, c), TC * r + c] = 1
         slots[224 + r, win_row(r, 0)] = 1
         slots[240 + r, win_row(r, 27)] = 1
-    halo = np.zeros((192, 256))
+    halo = np.zeros((160, 256))
     for line in range(2):
         for c in range(TC):
             for half in range(2):
@@ -61,8 +59,8 @@
     for r in range(TR):
         for c in range(2):
             for side in range(2):
-                halo[128 + 16 * (2 * side + c) + r + 2, 128 + 16 * side + 2 * r + c] = 1
-    halo2 = np.zeros((96, 256))
+                halo[128 + 8 * (2 * side + c) + r, 128 + 16 * side + 2 * r + c] = 1
+    halo2 = np.zeros((80, 256))
     for half in range(2):
         for c in range(TC):
             halo2[32 * half + c + 2, 32 * half + c + 2] = 1
@@ -71,7 +69,7 @@
             halo2[32 * half + 1 + 29 * side, 64 + 16 * (2 + 2 * half + side) + row] = 1
     for r in range(TR):
         for side in range(2):
-            halo2[64 + 16 * side + r, 64 + 16 * side + r] = 1
+            halo2[64 + 8 * side + r, 64 + 16 * side + r] = 1
     parts = dict(
         edge=edge, halo=halo, to_win=to_win, from_win=from_win, back_win=back_win,
         slots=slots, halo2=halo2,
@@ -136,7 +134,7 @@
     x_ref, cot_ref, cgain_ref, dw_ref, bgain_ref, ggain_ref,
     places_hbm, we_hbm, wp_hbm, bqkv_hbm, bout_hbm, bbias_hbm, gqkv_hbm, gout_hbm, gbias_hbm,
     out_ref, grad_ref,
-    places, we, wp, bqkv, bout, bbias, gqkv, gout, gbias, load_sem,
+    places, we, wp, bqkv, bout, bbias, gqkv, gout, gbias, load_sem, reach,
     stage, own, cat, edges, own2, cat2, halo_sem, halo2_sem,
     cot_send, cot_recv, fwd_send, fwd_recv, res_send, res_recv, gra_send, gra_recv, grid_sem,
     mixbuf, xhat0, scale0, normed0, normed1, slope_u, slope_p, pre_act, update,
@@ -163,17 +161,18 @@
         one.start()
     l_places, l_we, l_wp, l_bb, l_gb, l_bqkv, l_bout, l_gout, l_gqkv = loads
 
+    def around(step, rows=(-1, 0, 1), cols=(-1, 0, 1)):
+        for a in rows:
+            for b in cols:
+                if a or b:
+                    yield lax.rem(i + ROWS + step * a, ROWS), lax.rem(j + COLS + step * b, COLS)
+
+    def greet(sem, devices):
+        for device in devices:
+            pl.semaphore_signal(sem, inc=1, device_id=device, device_id_type=MESH)
+
     barrier = pltpu.get_barrier_semaphore()
-
-    def greet(step, carry):
-        other = lax.rem(me + step, ROWS * COLS)
-        pl.semaphore_signal(
-            barrier, inc=1, device_id=(lax.div(other, COLS), lax.rem(other, COLS)),
-            device_id_type=MESH,
-        )
-        return carry
-
-    lax.fori_loop(1, ROWS * COLS, greet, 0)
+    greet(barrier, around(1))
 
     def place(name, source):
         at, size = STARTS[name]
@@ -194,25 +193,82 @@
             ].astype(F32)
     cot_send[...] = mixbuf[0:784, :].reshape(LEN, 16, 128).astype(BF16)
 
-    def flip(bias, h):
-        square = jnp.concatenate(
-            [bias[pl.ds(h, LEN, stride=16), :], jnp.zeros((LEN, 128 - LEN), F32)], axis=1
-        )
-        square = jnp.concatenate([square, jnp.zeros((WPAD - LEN, 128), F32)], axis=0)
-        turned = square.T[0:WPAD]
-        key = lax.broadcasted_iota(jnp.int32, (WPAD, WPAD), 0)
-        return jnp.where(key < LEN, turned, -1e30)
-
-    def flip_all(bias, bias_t):
-        for g in range(4):
-            for h in range(2):
-                pair = [flip(bias, 4 * g + 2 * h + n) for n in range(2)]
-                bias_t[g, :, 128 * h : 128 * (h + 1)] = jnp.concatenate(pair, axis=1)
-
-    l_bb.wait()
-    flip_all(bbias, bias_b)
-    l_gb.wait()
-    flip_all(gbias, bias_g)
+    pl.semaphore_wait(barrier, 8)
+
+    north, south = lax.rem(i + ROWS - 1, ROWS), lax.rem(i + 1, ROWS)
+    west, east = lax.rem(j + COLS - 1, COLS), lax.rem(j + 1, COLS)
+
+    def swap(sems, parts):
+        copies = [
+            pltpu.make_async_remote_copy(
+                src_ref=src, dst_ref=dst, send_sem=sems.at[0, n], recv_sem=sems.at[1, n],
+                device_id=to, device_id_type=MESH,
+            )
+            for n, (src, dst, to) in enumerate(parts)
+        ]
+        for one in copies:
+            one.start()
+        return copies
+
+    w_cols, e_cols = edges.at[pl.ds(0, 16)], edges.at[pl.ds(16, 16)]
+    halo = swap(
+        halo_sem,
+        [
+            (own.at[pl.ds(0, 64)], cat.at[pl.ds(64, 64)], (north, j)),
+            (own.at[pl.ds(160, 64)], cat.at[pl.ds(0, 64)], (south, j)),
+            (e_cols, cat.at[pl.ds(128, 16)], (i, east)),
+            (w_cols, cat.at[pl.ds(144, 16)], (i, west)),
+            (e_cols, cat.at[pl.ds(160, 16)], (south, east)),
+            (w_cols, cat.at[pl.ds(176, 16)], (south, west)),
+            (e_cols, cat.at[pl.ds(192, 16)], (north, east)),
+            (w_cols, cat.at[pl.ds(208, 16)], (north, west)),
+        ],
+    )
+
+    def send_chunks(send, recv, sems, forward):
+        def body(c, carry):
+            a, b = lax.div(c, WIN), lax.rem(c, WIN)
+            if forward:
+                row, col = WIN * i + a, WIN * j + b
+                ti, tj = lax.rem(row, ROWS), lax.rem(col, COLS)
+                slot = lax.div(row, ROWS) * WIN + lax.div(col, COLS)
+            else:
+                row, col = ROWS * a + i, COLS * b + j
+                ti, tj = lax.div(row, WIN), lax.div(col, WIN)
+                slot = lax.rem(row, WIN) * WIN + lax.rem(col, WIN)
+            mine = jnp.logical_and(ti == i, tj == j)
+
+            @pl.when(mine)
+            def _():
+                pltpu.make_async_copy(send.at[c], recv.at[slot], sems.at[1]).start()
+
+            @pl.when(jnp.logical_not(mine))
+            def _():
+                pltpu.make_async_remote_copy(
+                    src_ref=send.at[c], dst_ref=recv.at[slot], send_sem=sems.at[0],
+                    recv_sem=sems.at[1], device_id=(ti, tj), device_id_type=MESH,
+                ).start()
+
+            return carry
+
+        lax.fori_loop(0, LEN, body, 0)
+
+    def wait_chunks(recv, sems):
+        pltpu.make_async_copy(recv, recv, sems.at[1]).wait()
+
+    def wait_sent(send, sems):
+        some = lax.rem(10 * i, ROWS) < WIN
+
+        @pl.when(some)
+        def _():
+            part = send.at[pl.ds(0, LEN - 1)]
+            pltpu.make_async_copy(part, part, sems.at[0]).wait()
+
+        @pl.when(jnp.logical_not(some))
+        def _():
+            pltpu.make_async_copy(send, send, sems.at[0]).wait()
+
+    greet(reach.at[0], around(1))
 
     xhat, scale = standardize(stage[...])
     xhat0[...] = xhat
@@ -220,19 +276,20 @@
     normed0[...] = (xhat * cgain_ref[...]).astype(BF16)
     l_we.wait()
 
-    def taps(at):
-        return [dw_ref[n : n + 1, pl.ds(at, CHUNK)] for n in range(9)]
-
-    def wide(ref, step, rows=slice(None)):
-        return jnp.concatenate([ref[step * TILES + n, rows, :] for n in range(TILES)], axis=1)
-
-    def put_wide(ref, step, rows, value):
-        for n in range(TILES):
-            ref[step * TILES + n, rows, :] = value[:, 128 * n : 128 * (n + 1)]
-
-    def add_wide(ref, step, first, value):
-        rows = slice(first, first + value.shape[0])
-        put_wide(ref, step, rows, wide(ref, step, rows) + value)
+    w = [dw_ref[n : n + 1, :] for n in range(9)]
+
+    def wide(ref, rows=slice(None)):
+        return jnp.concatenate([ref[n, rows, :] for n in range(ref.shape[0])], axis=1)
+
+    def put_wide(ref, rows, value):
+        for n in range(ref.shape[0]):
+            ref[n, rows, :] = value[:, 128 * n : 128 * (n + 1)]
+
+    def add_wide(ref, rows, value):
+        put_wide(ref, rows, wide(ref, rows) + value)
+
+    def column(first, count):
+        return pl.ds(first, count, stride=SW)
 
     def lines(x, first, last):
         return x[SW * first : SW * last]
@@ -241,12 +298,10 @@
         count = y[0].shape[0]
         return pltpu.roll(y[0], 1, 0) + y[1] + pltpu.roll(y[2], count - 1, 0)
 
-    def expand_own(step, carry):
-        at = pl.multiple_of(step * CHUNK, CHUNK)
-        e, slope = gelu_of(dot(normed0[...], we[:, pl.ds(at, CHUNK)]))
-        slope_u[:, pl.ds(at, CHUNK)] = slope
+    def expand_own():
+        e, slope = gelu_of(dot(normed0[...], we[...]))
+        put_wide(slope_u, slice(0, 224), slope)
         e = e.astype(BF16).astype(F32)
-        w = taps(at)
         y = []
         for b in range(3):
             t = [e * w[3 * a + b] for a in range(3)]
@@ -262,88 +317,39 @@
                     axis=0,
                 )
             )
-        put_wide(pre_act, step, slice(None), side_by_side(y))
-        return carry
-
-    lax.fori_loop(0, 1, expand_own, 0)
-    pl.semaphore_wait(barrier, ROWS * COLS - 1)
-
-    north, south = lax.rem(i + ROWS - 1, ROWS), lax.rem(i + 1, ROWS)
-    west, east = lax.rem(j + COLS - 1, COLS), lax.rem(j + 1, COLS)
-
-    def swap(sems, parts):
-        copies = [
-            pltpu.make_async_remote_copy(
-                src_ref=src, dst_ref=dst, send_sem=sems.at[0, n], recv_sem=sems.at[1, n],
-                device_id=to, device_id_type=MESH,
-            )
-            for n, (src, dst, to) in enumerate(parts)
-        ]
-        for one in copies:
-            one.start()
-        return copies
-
-    w_cols, e_cols = edges.at[pl.ds(0, 16)], edges.at[pl.ds(16, 16)]
-    halo = swap(
-        halo_sem,
-        [
-            (own.at[pl.ds(0, 64)], cat.at[pl.ds(64, 64)], (north, j)),
-            (own.at[pl.ds(160, 64)], cat.at[pl.ds(0, 64)], (south, j)),
-            (e_cols, cat.at[pl.ds(128, 16)], (i, east)),
-            (w_cols, cat.at[pl.ds(144, 16)], (i, west)),
-            (e_cols, cat.at[pl.ds(160, 16)], (south, east)),
-            (w_cols, cat.at[pl.ds(176, 16)], (south, west)),
-            (e_cols, cat.at[pl.ds(192, 16)], (north, east)),
-            (w_cols, cat.at[pl.ds(208, 16)], (north, west)),
-        ],
-    )
-
-    def send_chunks(send, recv, sems, forward):
-        def body(c, carry):
-            a, b = lax.div(c, WIN), lax.rem(c, WIN)
-            if forward:
-                row, col = WIN * i + a, WIN * j + b
-                ti, tj = lax.rem(row, ROWS), lax.rem(col, COLS)
-                slot = lax.div(row, ROWS) * WIN + lax.div(col, COLS)
-            else:
-                row, col = ROWS * a + i, COLS * b + j
-                ti, tj = lax.div(row, WIN), lax.div(col, WIN)
-                slot = lax.rem(row, WIN) * WIN + lax.rem(col, WIN)
-            mine = jnp.logical_and(ti == i, tj == j)
-
-            @pl.when(mine)
-            def _():
-                pltpu.make_async_copy(send.at[c], recv.at[slot], sems.at[1]).start()
-
-            @pl.when(jnp.logical_not(mine))
-            def _():
-                pltpu.make_async_remote_copy(
-                    src_ref=send.at[c], dst_ref=recv.at[slot], send_sem=sems.at[0],
-                    recv_sem=sems.at[1], device_id=(ti, tj), device_id_type=MESH,
-                ).start()
-
-            return carry
-
-        lax.fori_loop(0, LEN, body, 0)
-
-    def wait_chunks(recv, sems):
-        pltpu.make_async_copy(recv, recv, sems.at[1]).wait()
-
-    def wait_sent(send, sems):
-        some = lax.rem(10 * i, ROWS) < WIN
-
-        @pl.when(some)
-        def _():
-            part = send.at[pl.ds(0, LEN - 1)]
-            pltpu.make_async_copy(part, part, sems.at[0]).wait()
-
-        @pl.when(jnp.logical_not(some))
-        def _():
-            pltpu.make_async_copy(send, send, sems.at[0]).wait()
-
-    send_chunks(cot_send, cot_recv, grid_sem.at[0], True)
-
-    lax.fori_loop(1, FF // CHUNK, expand_own, 0)
+        put_wide(pre_act, slice(None), side_by_side(y))
+
+    expand_own()
+    pl.semaphore_wait(reach.at[0], 8)
+    greet(reach.at[1], around(2))
+
+    def flip(bias, h):
+        square = jnp.concatenate(
+            [bias[pl.ds(h, LEN, stride=16), :], jnp.zeros((LEN, 128 - LEN), F32)], axis=1
+        )
+        square = jnp.concatenate([square, jnp.zeros((WPAD - LEN, 128), F32)], axis=0)
+        turned = square.T[0:WPAD]
+        key = lax.broadcasted_iota(jnp.int32, (WPAD, WPAD), 0)
+        return jnp.where(key < LEN, turned, -1e30)
+
+    def flip_all(bias, bias_t):
+        for g in range(4):
+            for h in range(2):
+                pair = [flip(bias, 4 * g + 2 * h + n) for n in range(2)]
+                bias_t[g, :, 128 * h : 128 * (h + 1)] = jnp.concatenate(pair, axis=1)
+
+    l_bb.wait()
+    flip_all(bbias, bias_b)
+    l_gb.wait()
+    flip_all(gbias, bias_g)
+
+    branch, slope = gelu_of(wide(pre_act, slice(32, 256)))
+    put_wide(slope_p, slice(32, 256), slope)
+    l_wp.wait()
+    put_wide(update, slice(None), dot(branch.astype(BF16), wp[...]))
+
+    pl.semaphore_wait(reach.at[1], 8)
+    greet(reach.at[2], around(4, cols=(0,)))
 
     for one in halo:
         one.wait_recv()
@@ -359,50 +365,52 @@
         columns = jnp.where(at < 2 * strip + column, has_w, has_e)
         return jnp.where(at < 2 * strip, strips, columns)
 
-    xh = place("halo", cat[...]) * inside(192, 64, 32)
+    xh = place("halo", cat[...]) * inside(160, 64, 16)
     normed1[...] = (standardize(xh)[0] * cgain_ref[...]).astype(BF16)
-    update[...] = jnp.zeros_like(update)
-    l_wp.wait()
-
-    def add_column(ref, slot, count, step, value):
-        rows = pl.ds(slot, count, stride=SW)
-        put_wide(ref, step, rows, wide(ref, step, rows) + value[0:count])
-
-    def mbconv(step, carry):
-        at = pl.multiple_of(step * CHUNK, CHUNK)
-        here = pl.ds(at, CHUNK)
-        e, _ = gelu_of(dot(normed1[...], we[:, here]))
-        e = e.astype(BF16).astype(F32)
-        w = taps(at)
-        n0, n1, s0, s1 = (lines(e, n, n + 1) for n in range(4))
-        w0, w1, e0, e1 = (e[128 + 16 * n : 144 + 16 * n] for n in range(4))
-        around = [
-            (0, [n0 * w[b] + n1 * w[3 + b] for b in range(3)]),
-            (32, [n1 * w[b] for b in range(3)]),
-            (224, [s0 * w[6 + b] for b in range(3)]),
-            (256, [s0 * w[3 + b] + s1 * w[6 + b] for b in range(3)]),
-        ]
-        for first, y in around:
-            add_wide(pre_act, step, first, side_by_side(y))
-
-        def down(terms):
-            return terms[0] + pltpu.roll(terms[1], 15, 0) + pltpu.roll(terms[2], 14, 0)
-
-        sides = [
-            (1, [w0 * w[3 * a] + w1 * w[3 * a + 1] for a in range(3)]),
-            (2, [w1 * w[3 * a] for a in range(3)]),
-            (29, [e0 * w[3 * a + 2] for a in range(3)]),
-            (30, [e0 * w[3 * a + 1] + e1 * w[3 * a + 2] for a in range(3)]),
-        ]
-        for slot, terms in sides:
-            add_column(pre_act, slot, 9, step, down(terms))
-        branch, slope = gelu_of(wide(pre_act, step))
-        put_wide(slope_p, step, slice(None), slope)
-        update[...] += dot(branch[32:256].astype(BF16), wp[here, :])
-        return carry
-
-    lax.fori_loop(0, FF // CHUNK, mbconv, 0)
-    mixed = (stage[...] + update[...]).astype(BF16)
+    e, _ = gelu_of(dot(normed1[...], we[...]))
+    e = e.astype(BF16).astype(F32)
+    n0, n1, s0, s1 = (lines(e, n, n + 1) for n in range(4))
+    w0, w1, e0, e1 = (
+        pltpu.roll(
+            jnp.concatenate([e[128 + 8 * n : 136 + 8 * n], jnp.zeros((8, FF), F32)], axis=0), 2, 0
+        )
+        for n in range(4)
+    )
+    around = [
+        (0, [n0 * w[b] + n1 * w[3 + b] for b in range(3)]),
+        (32, [n1 * w[b] for b in range(3)]),
+        (224, [s0 * w[6 + b] for b in range(3)]),
+        (256, [s0 * w[3 + b] + s1 * w[6 + b] for b in range(3)]),
+    ]
+    for first, y in around:
+        add_wide(pre_act, slice(first, first + SW), side_by_side(y))
+    sides = [
+        (1, [w0 * w[3 * a] + w1 * w[3 * a + 1] for a in range(3)]),
+        (2, [w1 * w[3 * a] for a in range(3)]),
+        (29, [e0 * w[3 * a + 2] for a in range(3)]),
+        (30, [e0 * w[3 * a + 1] + e1 * w[3 * a + 2] for a in range(3)]),
+    ]
+    for slot, y in sides:
+        y = y[0] + pltpu.roll(y[1], 15, 0) + pltpu.roll(y[2], 14, 0)
+        add_wide(pre_act, column(slot, 9), y[0:9])
+
+    kept = []
+    for rows in [slice(0, 32), slice(32, 64), slice(224, 256), slice(256, 288)] + [
+        column(SW + slot, 8) for slot in (1, 2, 29, 30)
+    ]:
+        branch, slope = gelu_of(wide(pre_act, rows))
+        put_wide(slope_p, rows, slope)
+        kept.append(branch)
+    rim = jnp.concatenate([kept[1], kept[2], kept[5], kept[6]], axis=0).astype(BF16)
+
+    def put_rim(ref, value):
+        put_wide(ref, slice(0, 32), value[0:32])
+        put_wide(ref, slice(192, 224), value[32:64])
+        put_wide(ref, column(2, TR), value[64 : 64 + TR])
+        put_wide(ref, column(29, TR), value[72 : 72 + TR])
+
+    put_rim(update, dot(rim, wp[...]))
+    mixed = (stage[...] + wide(update)).astype(BF16)
     zwin[...] = place("to_win", mixed)
 
     root = HEAD_DIM**-0.5
@@ -485,7 +493,9 @@
     for k in range(4):
         mixbuf[pl.ds(k, 208, stride=4), :] = spatial[:, 128 * k : 128 * (k + 1)]
     fwd_send[...] = mixbuf[0:784, :].reshape(LEN, 16, 128).astype(BF16)
+    pl.semaphore_wait(reach.at[2], 2)
     send_chunks(fwd_send, fwd_recv, grid_sem.at[1], True)
+    send_chunks(cot_send, cot_recv, grid_sem.at[0], True)
 
     def to_windows(recv, target):
         mixbuf[0:784, :] = recv[...].astype(F32).reshape(784, 128)
@@ -505,17 +515,17 @@
 
     dgrid[...] = jnp.zeros_like(dgrid)
     zgrid[...] = jnp.zeros_like(zgrid)
+    l_gqkv.wait()
+
+    wait_chunks(fwd_recv, grid_sem.at[1])
+    to_windows(fwd_recv, zgrid)
+    project_in(zgrid[...], ggain_ref, gqkv, packed_g, xhat_g, scale_g)
+    attend(packed_g, bias_g, prob_g)
     wait_chunks(cot_recv, grid_sem.at[0])
     to_windows(cot_recv, dgrid)
     dout[...] = dgrid[...].astype(BF16)
     l_gout.wait()
     da[...] = dot_nt(dout[...], gout[...]).astype(BF16)
-    l_gqkv.wait()
-
-    wait_chunks(fwd_recv, grid_sem.at[1])
-    to_windows(fwd_recv, zgrid)
-    project_in(zgrid[...], ggain_ref, gqkv, packed_g, xhat_g, scale_g)
-    attend(packed_g, bias_g, prob_g)
     attend_back(packed_g, prob_g)
     dgrid[...] = project_back(gqkv, ggain_ref, xhat_g, scale_g).astype(F32)
     from_windows(dgrid, gra_send)
@@ -549,11 +559,9 @@
         ],
     )
 
-    def back_own(step, carry):
-        here = pl.ds(pl.multiple_of(step * CHUNK, CHUNK), CHUNK)
-        gp = dot_nt(own2[0:224, :], wp[here, :]).astype(BF16).astype(F32)
-        gp = gp * wide(slope_p, step, slice(32, 256))
-        w = taps(pl.multiple_of(step * CHUNK, CHUNK))
+    def back_own():
+        gp = dot_nt(own2[0:224, :], wp[...]).astype(BF16).astype(F32)
+        gp = gp * wide(slope_p, slice(32, 256))
         y = []
         for b in range(3):
             t = [gp * w[3 * a + 2 - b] for a in range(3)]
@@ -567,45 +575,40 @@
                     axis=0,
                 )
             )
-        put_wide(grad_e, step, slice(None), side_by_side(y))
-        return carry
-
-    lax.fori_loop(0, FF // CHUNK, back_own, 0)
-    update[...] = jnp.zeros_like(update)
+        put_wide(grad_e, slice(0, 224), side_by_side(y))
+
+    def back_hidden(rows):
+        return wide(grad_e, rows).astype(BF16).astype(F32) * wide(slope_u, rows)
+
+    back_own()
+    put_wide(update, slice(None), dot_nt(back_hidden(slice(0, 224)).astype(BF16), we[...]))
     wait_chunks(res_recv, grid_sem.at[2])
     out_ref[...] = res_recv[...]
 
     for one in halo2:
         one.wait_recv()
-    gm = place("halo2", cat2[...]) * inside(96, 32, 16)
+    gm = place("halo2", cat2[...]) * inside(80, 32, 8)
     halo_grad[...] = gm.astype(BF16)
 
-    def mbconv_back(step, carry):
-        at = pl.multiple_of(step * CHUNK, CHUNK)
-        here = pl.ds(at, CHUNK)
-        gp = dot_nt(halo_grad[...], wp[here, :]).astype(BF16).astype(F32)
-        w = taps(at)
-
-        north_gp = gp[0:32] * wide(slope_p, step, slice(0, 32))
-        south_gp = gp[32:64] * wide(slope_p, step, slice(256, 288))
-        west_gp = gp[64:72] * wide(slope_p, step, pl.ds(SW + 1, 8, stride=SW))
-        east_gp = gp[80:88] * wide(slope_p, step, pl.ds(SW + 30, 8, stride=SW))
-        add_wide(grad_e, step, 0, side_by_side([north_gp * w[8 - b] for b in range(3)]))
-        add_wide(grad_e, step, 192, side_by_side([south_gp * w[2 - b] for b in range(3)]))
-
-        def down(x, b):
-            return (
-                pltpu.roll(x * w[b], 7, 0) + x * w[3 + b] + pltpu.roll(x * w[6 + b], 1, 0)
-            )
-
-        add_column(grad_e, 2, 7, step, down(west_gp, 2))
-        add_column(grad_e, 29, 7, step, down(east_gp, 0))
-        gh = wide(grad_e, step).astype(BF16).astype(F32) * slope_u[:, here]
-        update[...] += dot_nt(gh.astype(BF16), we[:, here])
-        return carry
-
-    lax.fori_loop(0, FF // CHUNK, mbconv_back, 0)
-    dn = update[...].astype(BF16).astype(F32)
+    gp = dot_nt(halo_grad[...], wp[...]).astype(BF16).astype(F32)
+    north_gp = gp[0:32] * wide(slope_p, slice(0, 32))
+    south_gp = gp[32:64] * wide(slope_p, slice(256, 288))
+    west_gp = gp[64:72] * wide(slope_p, column(SW + 1, 8))
+    east_gp = gp[72:80] * wide(slope_p, column(SW + 30, 8))
+    add_wide(grad_e, slice(0, 32), side_by_side([north_gp * w[8 - b] for b in range(3)]))
+    add_wide(grad_e, slice(192, 224), side_by_side([south_gp * w[2 - b] for b in range(3)]))
+    for slot, x, b in ((2, west_gp, 2), (29, east_gp, 0)):
+        y = pltpu.roll(x * w[b], 7, 0) + x * w[3 + b] + pltpu.roll(x * w[6 + b], 1, 0)
+        add_wide(grad_e, column(slot, TR), y[0:TR])
+    rim = jnp.concatenate(
+        [
+            back_hidden(rows)
+            for rows in (slice(0, 32), slice(192, 224), column(2, 8), column(29, 8))
+        ],
+        axis=0,
+    ).astype(BF16)
+    put_rim(update, dot_nt(rim, we[...]))
+    dn = wide(update).astype(BF16).astype(F32)
     dx = standardize_back(dn * cgain_ref[...], xhat0[...], scale0[...])
     stage[...] = stage[...] + dx.astype(BF16).astype(F32)
     for r in range(TR):
@@ -648,20 +651,20 @@
         pltpu.VMEM(PLACES.shape, BF16), pltpu.VMEM((D, FF), BF16), pltpu.VMEM((FF, D), BF16),
         pltpu.VMEM((D, 3 * D), BF16), pltpu.VMEM((D, D), BF16), bias,
         pltpu.VMEM((D, 3 * D), BF16), pltpu.VMEM((D, D), BF16), bias,
-        pltpu.SemaphoreType.DMA((9,)),
+        pltpu.SemaphoreType.DMA((9,)), pltpu.SemaphoreType.REGULAR((3,)),
         pltpu.VMEM((224, D), F32), pltpu.VMEM((224, D), BF16), pltpu.VMEM((224, D), BF16),
         pltpu.VMEM((32, D), BF16), pltpu.VMEM((256, D), BF16), pltpu.VMEM((160, D), BF16),
         pltpu.SemaphoreType.DMA((2, 8)), pltpu.SemaphoreType.DMA((2, 8)),
         chunks, chunks, chunks, chunks, chunks, chunks, chunks, chunks,
         pltpu.SemaphoreType.DMA((4, 2)),
         pltpu.VMEM((832, 128), F32), pltpu.VMEM((224, D), F32), pltpu.VMEM((224, 1), F32),
-        pltpu.VMEM((224, D), BF16), pltpu.VMEM((192, D), BF16), pltpu.VMEM((224, FF), F32),
-        pltpu.VMEM((FF // 128, 288, 128), F32), pltpu.VMEM((FF // 128, 288, 128), F32),
-        pltpu.VMEM((224, D), F32),
+        pltpu.VMEM((224, D), BF16), pltpu.VMEM((160, D), BF16),
+        pltpu.VMEM((FF // 128, 256, 128), F32), pltpu.VMEM((FF // 128, 288, 128), F32),
+        pltpu.VMEM((FF // 128, 288, 128), F32), pltpu.VMEM((D // 128, 224, 128), F32),
         bias_t, bias_t, win_f32, packed, win_f32, scale, prob, win_bf16,
         win_f32, win_f32, packed, win_f32, scale, prob, win_bf16, win_bf16, packed,
-        pltpu.VMEM((NWIN, 4, WPAD, 256), BF16), pltpu.VMEM((96, D), BF16),
-        pltpu.VMEM((FF // 128, 224, 128), F32),
+        pltpu.VMEM((NWIN, 4, WPAD, 256), BF16), pltpu.VMEM((80, D), BF16),
+        pltpu.VMEM((FF // 128, 256, 128), F32),
     ]
     result, grad = pl.pallas_call(
         kernel,

time: 53.5 us -> 52.8 us (0.987)
  Pallas kernels: 52.7 us -> 52 us
    pallas_call x1, Pallas kernels: 50.8 us -> 50.1 us  [local(): pl.pallas_call(kernel, out_shape=(jax.ShapeDtypeStruct((LEN, 16, 128), BF...]
where the time goes in v5:
time: 52.8 us; the launch traced here: 52.6 us
  Pallas kernels  52 us (98%)
  between operations  0.64 us (1%)
    pallas_call x1, Pallas kernels, local(): pl.pallas_call(kernel, out_shape=(jax.ShapeDtypeStruct((LEN, 16, 128), BF...  50.1 us
    pallas_call x1, Pallas kernels, local(): pl.pallas_call(finish, out_shape=(tokens, tokens), in_specs=[vmem] * 2, o...  1.87 us

profile of v5, /device:TPU:0, one launch (start us, length us, event | category | flops | bytes accessed | tf_op | source)
XLA Modules:
  0.0 52.6 jit_solution(3035674192325810212)
XLA Ops:
  0.6 50.1 %mbconv_attention.1 = (bf16[49,16,128]{2,1,0:T(8,128)(2,1)}, bf16[7,28,512]{2,1,0:T(8,128)(2,1)}) custom-call(bf16[7,28,512]{2,1,0:T(8,128)(2,1)} %x_ref.1, bf16[7,28,512]{2,1,0:T(8,128)(2,1)} %cot_ref.1, f32[1,512]{1,0:T(1,128)} %bitcast.11, f32[9,2048]{1,0:T(8,128)} %dw_ref.1, f32[1,512]{1,0:T(1,128)} %bitcast.12, f32[1,512]{1,0:T(1,128)} %bitcast.13, ...), custom_call_target="tpu_custom_call" | custom-call | tf_op jit(solution)/shard_map/mbconv_attention/pallas_call | solution.py:669
  50.8 1.9 %finish.1 = (bf16[7,28,512]{2,1,0:T(8,128)(2,1)}, bf16[7,28,512]{2,1,0:T(8,128)(2,1)}) custom-call(bf16[49,16,128]{2,1,0:T(8,128)(2,1)} %get-tuple-element.4.chunks_ref, bf16[7,28,512]{2,1,0:T(8,128)(2,1)} %get-tuple-element.5.kept_ref), custom_call_target="tpu_custom_call" | custom-call | tf_op jit(solution)/shard_map/finish/pallas_call | solution.py:684

commit v6 on v5

--- a/solution.py
+++ b/solution.py
@@ -60,7 +60,7 @@
         for c in range(2):
             for side in range(2):
                 halo[128 + 8 * (2 * side + c) + r, 128 + 16 * side + 2 * r + c] = 1
-    halo2 = np.zeros((80, 256))
+    halo2 = np.zeros((96, 256))
     for half in range(2):
         for c in range(TC):
             halo2[32 * half + c + 2, 32 * half + c + 2] = 1
@@ -69,7 +69,7 @@
             halo2[32 * half + 1 + 29 * side, 64 + 16 * (2 + 2 * half + side) + row] = 1
     for r in range(TR):
         for side in range(2):
-            halo2[64 + 8 * side + r, 64 + 16 * side + r] = 1
+            halo2[64 + 16 * side + r + 1, 64 + 16 * side + r] = 1
     parts = dict(
         edge=edge, halo=halo, to_win=to_win, from_win=from_win, back_win=back_win,
         slots=slots, halo2=halo2,
@@ -140,6 +140,7 @@
     mixbuf, xhat0, scale0, normed0, normed1, slope_u, slope_p, pre_act, update,
     bias_b, bias_g, zwin, packed_b, xhat_b, scale_b, prob_b, att,
     zgrid, dgrid, packed_g, xhat_g, scale_g, prob_g, dout, da, dpk, dscore, halo_grad, grad_e,
+    cols_pre, cols_slope, cols_u, cols_e, halo_e,
 ):
     i, j = lax.axis_index("rows"), lax.axis_index("cols")
     me = i * COLS + j
@@ -285,11 +286,18 @@
         for n in range(ref.shape[0]):
             ref[n, rows, :] = value[:, 128 * n : 128 * (n + 1)]
 
-    def add_wide(ref, rows, value):
-        put_wide(ref, rows, wide(ref, rows) + value)
-
     def column(first, count):
         return pl.ds(first, count, stride=SW)
+
+    def beside(strip, ends):
+        at = lax.broadcasted_iota(jnp.int32, (8, 1), 0)
+        first, last = strip[0:8], strip[24:32]
+        for slot, row in ends:
+            if slot < 8:
+                first += jnp.where(at == slot, 1.0, 0.0) * row
+            else:
+                last += jnp.where(at == slot - 24, 1.0, 0.0) * row
+        return jnp.concatenate([first, strip[8:24], last], axis=0)
 
     def lines(x, first, last):
         return x[SW * first : SW * last]
@@ -351,6 +359,10 @@
     pl.semaphore_wait(reach.at[1], 8)
     greet(reach.at[2], around(4, cols=(0,)))
 
+    cols_pre[...] = jnp.zeros_like(cols_pre)
+    for n, slot in enumerate((1, 2, 29, 30)):
+        cols_pre[n, 0:9, :] = wide(pre_act, column(slot, 9))
+
     for one in halo:
         one.wait_recv()
     has_n, has_s, has_w, has_e = (
@@ -369,47 +381,63 @@
     normed1[...] = (standardize(xh)[0] * cgain_ref[...]).astype(BF16)
     e, _ = gelu_of(dot(normed1[...], we[...]))
     e = e.astype(BF16).astype(F32)
-    n0, n1, s0, s1 = (lines(e, n, n + 1) for n in range(4))
-    w0, w1, e0, e1 = (
-        pltpu.roll(
-            jnp.concatenate([e[128 + 8 * n : 136 + 8 * n], jnp.zeros((8, FF), F32)], axis=0), 2, 0
-        )
-        for n in range(4)
-    )
-    around = [
-        (0, [n0 * w[b] + n1 * w[3 + b] for b in range(3)]),
-        (32, [n1 * w[b] for b in range(3)]),
-        (224, [s0 * w[6 + b] for b in range(3)]),
-        (256, [s0 * w[3 + b] + s1 * w[6 + b] for b in range(3)]),
+    halo_e[...] = e
+
+    def side(n):
+        x = halo_e[128 + 8 * n : 136 + 8 * n, :]
+        return pltpu.roll(jnp.concatenate([x, jnp.zeros((8, FF), F32)], axis=0), 2, 0)
+
+    def downwards(terms):
+        return terms[0] + pltpu.roll(terms[1], 15, 0) + pltpu.roll(terms[2], 14, 0)
+
+    def strip(line, y, ends):
+        ends = [(slot, x[line : line + 1]) for slot, x in ends]
+        rows = slice(SW * line, SW * (line + 1))
+        return wide(pre_act, rows) + beside(side_by_side(y), ends)
+
+    left = downwards([side(1) * w[3 * a] for a in range(3)])
+    right = downwards([side(2) * w[3 * a + 2] for a in range(3)])
+    ends = [(2, left), (29, right)]
+    rim = [
+        strip(1, [lines(e, 1, 2) * w[b] for b in range(3)], ends),
+        strip(7, [lines(e, 2, 3) * w[6 + b] for b in range(3)], ends),
+        cols_pre[1] + left,
+        cols_pre[2] + right,
     ]
-    for first, y in around:
-        add_wide(pre_act, slice(first, first + SW), side_by_side(y))
-    sides = [
-        (1, [w0 * w[3 * a] + w1 * w[3 * a + 1] for a in range(3)]),
-        (2, [w1 * w[3 * a] for a in range(3)]),
-        (29, [e0 * w[3 * a + 2] for a in range(3)]),
-        (30, [e0 * w[3 * a + 1] + e1 * w[3 * a + 2] for a in range(3)]),
-    ]
-    for slot, y in sides:
-        y = y[0] + pltpu.roll(y[1], 15, 0) + pltpu.roll(y[2], 14, 0)
-        add_wide(pre_act, column(slot, 9), y[0:9])
-
-    kept = []
-    for rows in [slice(0, 32), slice(32, 64), slice(224, 256), slice(256, 288)] + [
-        column(SW + slot, 8) for slot in (1, 2, 29, 30)
-    ]:
-        branch, slope = gelu_of(wide(pre_act, rows))
-        put_wide(slope_p, rows, slope)
-        kept.append(branch)
-    rim = jnp.concatenate([kept[1], kept[2], kept[5], kept[6]], axis=0).astype(BF16)
-
-    def put_rim(ref, value):
+    rim = jnp.concatenate([gelu_of(x)[0] for x in rim], axis=0).astype(BF16)
+
+    def halo_slopes():
+        n0, n1, s0, s1 = (halo_e[SW * n : SW * (n + 1), :] for n in range(4))
+        w0, w1, e0, e1 = (side(n) for n in range(4))
+        sides = [
+            downwards([w0 * w[3 * a] + w1 * w[3 * a + 1] for a in range(3)]),
+            downwards([w1 * w[3 * a] for a in range(3)]),
+            downwards([e0 * w[3 * a + 2] for a in range(3)]),
+            downwards([e0 * w[3 * a + 1] + e1 * w[3 * a + 2] for a in range(3)]),
+        ]
+        ends = list(zip((1, 2, 29, 30), sides))
+        for line, y in (
+            (0, [n0 * w[b] + n1 * w[3 + b] for b in range(3)]),
+            (1, [n1 * w[b] for b in range(3)]),
+            (7, [s0 * w[6 + b] for b in range(3)]),
+            (8, [s0 * w[3 + b] + s1 * w[6 + b] for b in range(3)]),
+        ):
+            slope = gelu_of(strip(line, y, ends))[1]
+            put_wide(slope_p, slice(SW * line, SW * (line + 1)), slope)
+        for n, x in enumerate(sides):
+            cols_slope[n] = gelu_of(cols_pre[n] + x)[1]
+        for n, slot in enumerate((1, 2, 29, 30)):
+            put_wide(slope_p, column(2 * SW + slot, 5), cols_slope[n, 2:7, :])
+        for n, slot in ((0, 1), (3, 30)):
+            cols_slope[n, 1:8, :] = wide(slope_p, column(SW + slot, TR))
+
+    def put_rim(ref, value, first):
+        put_wide(ref, column(2, TR), value[64 + first : 64 + first + TR])
+        put_wide(ref, column(29, TR), value[80 + first : 80 + first + TR])
         put_wide(ref, slice(0, 32), value[0:32])
         put_wide(ref, slice(192, 224), value[32:64])
-        put_wide(ref, column(2, TR), value[64 : 64 + TR])
-        put_wide(ref, column(29, TR), value[72 : 72 + TR])
-
-    put_rim(update, dot(rim, wp[...]))
+
+    put_rim(update, dot(rim, wp[...]), 1)
     mixed = (stage[...] + wide(update)).astype(BF16)
     zwin[...] = place("to_win", mixed)
 
@@ -496,6 +524,12 @@
     pl.semaphore_wait(reach.at[2], 2)
     send_chunks(fwd_send, fwd_recv, grid_sem.at[1], True)
     send_chunks(cot_send, cot_recv, grid_sem.at[0], True)
+
+    halo_slopes()
+    cols_u[...] = jnp.zeros_like(cols_u)
+    cols_e[...] = jnp.zeros_like(cols_e)
+    for n, slot in enumerate((2, 29)):
+        cols_u[n, 0:TR, :] = wide(slope_u, column(slot, TR))
 
     def to_windows(recv, target):
         mixbuf[0:784, :] = recv[...].astype(F32).reshape(784, 128)
@@ -581,33 +615,43 @@
         return wide(grad_e, rows).astype(BF16).astype(F32) * wide(slope_u, rows)
 
     back_own()
+    for n, slot in enumerate((2, 29)):
+        cols_e[n, 0:TR, :] = wide(grad_e, column(slot, TR))
     put_wide(update, slice(None), dot_nt(back_hidden(slice(0, 224)).astype(BF16), we[...]))
     wait_chunks(res_recv, grid_sem.at[2])
     out_ref[...] = res_recv[...]
 
     for one in halo2:
         one.wait_recv()
-    gm = place("halo2", cat2[...]) * inside(80, 32, 8)
+    gm = place("halo2", cat2[...]) * inside(96, 32, 16)
     halo_grad[...] = gm.astype(BF16)
 
     gp = dot_nt(halo_grad[...], wp[...]).astype(BF16).astype(F32)
     north_gp = gp[0:32] * wide(slope_p, slice(0, 32))
     south_gp = gp[32:64] * wide(slope_p, slice(256, 288))
-    west_gp = gp[64:72] * wide(slope_p, column(SW + 1, 8))
-    east_gp = gp[72:80] * wide(slope_p, column(SW + 30, 8))
-    add_wide(grad_e, slice(0, 32), side_by_side([north_gp * w[8 - b] for b in range(3)]))
-    add_wide(grad_e, slice(192, 224), side_by_side([south_gp * w[2 - b] for b in range(3)]))
-    for slot, x, b in ((2, west_gp, 2), (29, east_gp, 0)):
-        y = pltpu.roll(x * w[b], 7, 0) + x * w[3 + b] + pltpu.roll(x * w[6 + b], 1, 0)
-        add_wide(grad_e, column(slot, TR), y[0:TR])
-    rim = jnp.concatenate(
-        [
-            back_hidden(rows)
-            for rows in (slice(0, 32), slice(192, 224), column(2, 8), column(29, 8))
-        ],
-        axis=0,
-    ).astype(BF16)
-    put_rim(update, dot_nt(rim, we[...]))
+    sides = []
+    for x, b in ((gp[64:80] * cols_slope[0], 2), (gp[80:96] * cols_slope[3], 0)):
+        sides.append(
+            pltpu.roll(x * w[b], 14, 0) + pltpu.roll(x * w[3 + b], 15, 0) + x * w[6 + b]
+        )
+
+    def hidden(grad, slope):
+        return grad.astype(BF16).astype(F32) * slope
+
+    rim = []
+    for line, y in (
+        (0, [north_gp * w[8 - b] for b in range(3)]),
+        (6, [south_gp * w[2 - b] for b in range(3)]),
+    ):
+        rows = slice(SW * line, SW * (line + 1))
+        ends = [(slot, x[line : line + 1]) for slot, x in zip((2, 29), sides)]
+        rim.append(
+            hidden(wide(grad_e, rows) + beside(side_by_side(y), ends), wide(slope_u, rows))
+        )
+    for n, x in enumerate(sides):
+        rim.append(hidden(cols_e[n] + x, cols_u[n]))
+    rim = jnp.concatenate(rim, axis=0).astype(BF16)
+    put_rim(update, dot_nt(rim, we[...]), 0)
     dn = wide(update).astype(BF16).astype(F32)
     dx = standardize_back(dn * cgain_ref[...], xhat0[...], scale0[...])
     stage[...] = stage[...] + dx.astype(BF16).astype(F32)
@@ -663,8 +707,10 @@
         pltpu.VMEM((FF // 128, 288, 128), F32), pltpu.VMEM((D // 128, 224, 128), F32),
         bias_t, bias_t, win_f32, packed, win_f32, scale, prob, win_bf16,
         win_f32, win_f32, packed, win_f32, scale, prob, win_bf16, win_bf16, packed,
-        pltpu.VMEM((NWIN, 4, WPAD, 256), BF16), pltpu.VMEM((80, D), BF16),
+        pltpu.VMEM((NWIN, 4, WPAD, 256), BF16), pltpu.VMEM((96, D), BF16),
         pltpu.VMEM((FF // 128, 256, 128), F32),
+        pltpu.VMEM((4, 16, FF), F32), pltpu.VMEM((4, 16, FF), F32),
+        pltpu.VMEM((2, 16, FF), F32), pltpu.VMEM((2, 16, FF), F32), pltpu.VMEM((160, FF), F32),
     ]
     result, grad = pl.pallas_call(
         kernel,

time: 52.8 us -> 51.8 us (0.981)
  Pallas kernels: 52 us -> 51 us
    pallas_call x1, Pallas kernels: 50.1 us -> 49.1 us  [local(): pl.pallas_call(kernel, out_shape=(jax.ShapeDtypeStruct((LEN, 16, 128), BF...]
where the time goes in v6:
time: 51.8 us; the launch traced here: 51.6 us
  Pallas kernels  51 us (98%)
  between operations  0.64 us (1%)
    pallas_call x1, Pallas kernels, local(): pl.pallas_call(kernel, out_shape=(jax.ShapeDtypeStruct((LEN, 16, 128), BF...  49.1 us
    pallas_call x1, Pallas kernels, local(): pl.pallas_call(finish, out_shape=(tokens, tokens), in_specs=[vmem] * 2, o...  1.87 us

profile of v6, /device:TPU:0, one launch (start us, length us, event | category | flops | bytes accessed | tf_op | source)
XLA Modules:
  0.0 51.6 jit_solution(14826880674267787780)
XLA Ops:
  0.6 49.1 %mbconv_attention.1 = (bf16[49,16,128]{2,1,0:T(8,128)(2,1)}, bf16[7,28,512]{2,1,0:T(8,128)(2,1)}) custom-call(bf16[7,28,512]{2,1,0:T(8,128)(2,1)} %x_ref.1, bf16[7,28,512]{2,1,0:T(8,128)(2,1)} %cot_ref.1, f32[1,512]{1,0:T(1,128)} %bitcast.11, f32[9,2048]{1,0:T(8,128)} %dw_ref.1, f32[1,512]{1,0:T(1,128)} %bitcast.12, f32[1,512]{1,0:T(1,128)} %bitcast.13, ...), custom_call_target="tpu_custom_call" | custom-call | tf_op jit(solution)/shard_map/mbconv_attention/pallas_call | solution.py:715
  49.7 1.9 %finish.1 = (bf16[7,28,512]{2,1,0:T(8,128)(2,1)}, bf16[7,28,512]{2,1,0:T(8,128)(2,1)}) custom-call(bf16[49,16,128]{2,1,0:T(8,128)(2,1)} %get-tuple-element.4.chunks_ref, bf16[7,28,512]{2,1,0:T(8,128)(2,1)} %get-tuple-element.5.kept_ref), custom_call_target="tpu_custom_call" | custom-call | tf_op jit(solution)/shard_map/finish/pallas_call | solution.py:730

commit v7 on v6

--- a/solution.py
+++ b/solution.py
@@ -28,15 +28,11 @@
 
 
 def placements():
-    edge = np.zeros((32, 256))
     slots = np.zeros((256, 256))
     to_win = np.zeros((256, 256))
     from_win = np.zeros((208, 256))
     back_win = np.zeros((256, 256))
     for r in range(TR):
-        for c in range(2):
-            edge[2 * r + c, SW * r + c + 2] = 1
-            edge[16 + 2 * r + c, SW * r + c + 28] = 1
         for c in range(TC):
             to_win[win_row(r, c), SW * r + c + 2] = 1
             slots[SW * r + c + 2, win_row(r, c)] = 1
@@ -71,7 +67,7 @@
         for side in range(2):
             halo2[64 + 16 * side + r + 1, 64 + 16 * side + r] = 1
     parts = dict(
-        edge=edge, halo=halo, to_win=to_win, from_win=from_win, back_win=back_win,
+        halo=halo, to_win=to_win, from_win=from_win, back_win=back_win,
         slots=slots, halo2=halo2,
     )
     starts, at = {}, 0
@@ -131,10 +127,11 @@
 
 
 def kernel(
-    x_ref, cot_ref, cgain_ref, dw_ref, bgain_ref, ggain_ref,
+    x_hbm, cot_hbm, cgain_hbm, dw_hbm, bgain_hbm, ggain_hbm,
     places_hbm, we_hbm, wp_hbm, bqkv_hbm, bout_hbm, bbias_hbm, gqkv_hbm, gout_hbm, gbias_hbm,
     out_ref, grad_ref,
     places, we, wp, bqkv, bout, bbias, gqkv, gout, gbias, load_sem, reach,
+    x_ref, cot_ref, cgain_ref, dw_ref, bgain_ref, ggain_ref, rims,
     stage, own, cat, edges, own2, cat2, halo_sem, halo2_sem,
     cot_send, cot_recv, fwd_send, fwd_recv, res_send, res_recv, gra_send, gra_recv, grid_sem,
     mixbuf, xhat0, scale0, normed0, normed1, slope_u, slope_p, pre_act, update,
@@ -145,6 +142,19 @@
     i, j = lax.axis_index("rows"), lax.axis_index("cols")
     me = i * COLS + j
 
+    def around(step, rows=(-1, 0, 1), cols=(-1, 0, 1)):
+        for a in rows:
+            for b in cols:
+                if a or b:
+                    yield lax.rem(i + ROWS + step * a, ROWS), lax.rem(j + COLS + step * b, COLS)
+
+    def greet(sem, devices):
+        for device in devices:
+            pl.semaphore_signal(sem, inc=1, device_id=device, device_id_type=MESH)
+
+    barrier = pltpu.get_barrier_semaphore()
+    greet(barrier, around(1))
+
     def load(index, src, dst):
         return pltpu.make_async_copy(src, dst, load_sem.at[index])
 
@@ -152,7 +162,9 @@
         load(n, src, dst)
         for n, (src, dst) in enumerate(
             [
-                (places_hbm, places), (we_hbm, we), (wp_hbm, wp), (bbias_hbm, bbias),
+                (x_hbm, x_ref), (places_hbm, places), (cgain_hbm, cgain_ref), (dw_hbm, dw_ref),
+                (we_hbm, we), (cot_hbm, cot_ref), (wp_hbm, wp), (bgain_hbm, bgain_ref),
+                (ggain_hbm, ggain_ref), (bbias_hbm, bbias),
                 (gbias_hbm, gbias), (bqkv_hbm, bqkv), (bout_hbm, bout),
                 (gout_hbm, gout), (gqkv_hbm, gqkv),
             ]
@@ -160,39 +172,23 @@
     ]
     for one in loads:
         one.start()
-    l_places, l_we, l_wp, l_bb, l_gb, l_bqkv, l_bout, l_gout, l_gqkv = loads
-
-    def around(step, rows=(-1, 0, 1), cols=(-1, 0, 1)):
-        for a in rows:
-            for b in cols:
-                if a or b:
-                    yield lax.rem(i + ROWS + step * a, ROWS), lax.rem(j + COLS + step * b, COLS)
-
-    def greet(sem, devices):
-        for device in devices:
-            pl.semaphore_signal(sem, inc=1, device_id=device, device_id_type=MESH)
-
-    barrier = pltpu.get_barrier_semaphore()
-    greet(barrier, around(1))
+    l_x, l_places, l_cgain, l_dw, l_we, l_cot, l_wp, l_bgain, l_ggain, l_bb = loads[:10]
+    l_gb, l_bqkv, l_bout, l_gout, l_gqkv = loads[10:]
 
     def place(name, source):
         at, size = STARTS[name]
         return dot(places[at : at + size, 0 : source.shape[0]], source)
 
     stage[...] = jnp.zeros_like(stage)
+    rims[...] = jnp.zeros_like(rims)
+    l_x.wait()
     for r in range(TR):
         stage[SW * r + 2 : SW * r + 2 + TC, :] = x_ref[r].astype(F32)
+    for r in range(TR):
+        rims[2 * r : 2 * r + 2, :] = stage[SW * r + 2 : SW * r + 4, :]
+        rims[16 + 2 * r : 18 + 2 * r, :] = stage[SW * r + 28 : SW * r + 30, :]
     own[...] = stage[...].astype(BF16)
-    l_places.wait()
-    edges[...] = place("edge", own[...]).astype(BF16)
-
-    mixbuf[...] = jnp.zeros_like(mixbuf)
-    for r in range(TR):
-        for k in range(4):
-            mixbuf[pl.ds(112 * r + k, TC, stride=4), :] = cot_ref[
-                r, :, 128 * k : 128 * (k + 1)
-            ].astype(F32)
-    cot_send[...] = mixbuf[0:784, :].reshape(LEN, 16, 128).astype(BF16)
+    edges[...] = rims[...].astype(BF16)
 
     pl.semaphore_wait(barrier, 8)
 
@@ -270,6 +266,17 @@
             pltpu.make_async_copy(send, send, sems.at[0]).wait()
 
     greet(reach.at[0], around(1))
+    l_places.wait()
+    l_cgain.wait()
+    l_dw.wait()
+    l_cot.wait()
+    mixbuf[...] = jnp.zeros_like(mixbuf)
+    for r in range(TR):
+        for k in range(4):
+            mixbuf[pl.ds(112 * r + k, TC, stride=4), :] = cot_ref[
+                r, :, 128 * k : 128 * (k + 1)
+            ].astype(F32)
+    cot_send[...] = mixbuf[0:784, :].reshape(LEN, 16, 128).astype(BF16)
 
     xhat, scale = standardize(stage[...])
     xhat0[...] = xhat
@@ -512,6 +519,8 @@
         return (dout[...].astype(F32) + dx.astype(BF16).astype(F32)).astype(BF16)
 
     l_bqkv.wait()
+    l_bgain.wait()
+    l_ggain.wait()
     project_in(zwin[...], bgain_ref, bqkv, packed_b, xhat_b, scale_b)
     attend(packed_b, bias_b, prob_b)
     l_bout.wait()
@@ -695,7 +704,10 @@
         pltpu.VMEM(PLACES.shape, BF16), pltpu.VMEM((D, FF), BF16), pltpu.VMEM((FF, D), BF16),
         pltpu.VMEM((D, 3 * D), BF16), pltpu.VMEM((D, D), BF16), bias,
         pltpu.VMEM((D, 3 * D), BF16), pltpu.VMEM((D, D), BF16), bias,
-        pltpu.SemaphoreType.DMA((9,)), pltpu.SemaphoreType.REGULAR((3,)),
+        pltpu.SemaphoreType.DMA((15,)), pltpu.SemaphoreType.REGULAR((3,)),
+        pltpu.VMEM((TR, TC, D), BF16), pltpu.VMEM((TR, TC, D), BF16), pltpu.VMEM((1, D), F32),
+        pltpu.VMEM((9, FF), F32), pltpu.VMEM((1, D), F32), pltpu.VMEM((1, D), F32),
+        pltpu.VMEM((32, D), F32),
         pltpu.VMEM((224, D), F32), pltpu.VMEM((224, D), BF16), pltpu.VMEM((224, D), BF16),
         pltpu.VMEM((32, D), BF16), pltpu.VMEM((256, D), BF16), pltpu.VMEM((160, D), BF16),
         pltpu.SemaphoreType.DMA((2, 8)), pltpu.SemaphoreType.DMA((2, 8)),
@@ -715,7 +727,7 @@
     result, grad = pl.pallas_call(
         kernel,
         out_shape=(jax.ShapeDtypeStruct((LEN, 16, 128), BF16), tokens),
-        in_specs=[vmem] * 6 + [hbm] * 9,
+        in_specs=[hbm] * 15,
         out_specs=(vmem, vmem),
         scratch_shapes=scratch,
         compiler_params=pltpu.CompilerParams(

time: 51.8 us -> 50.8 us (0.981)
  Pallas kernels: 51 us -> 49.9 us
    pallas_call x1, Pallas kernels: 49.1 us -> 48.1 us  [local(): pl.pallas_call(kernel, out_shape=(jax.ShapeDtypeStruct((LEN, 16, 128), BF...]
where the time goes in v7:
time: 50.8 us; the launch traced here: 50.6 us
  Pallas kernels  49.9 us (98%)
  between operations  0.64 us (1%)
    pallas_call x1, Pallas kernels, local(): pl.pallas_call(kernel, out_shape=(jax.ShapeDtypeStruct((LEN, 16, 128), BF...  48.1 us
    pallas_call x1, Pallas kernels, local(): pl.pallas_call(finish, out_shape=(tokens, tokens), in_specs=[vmem] * 2, o...  1.87 us

profile of v7, /device:TPU:0, one launch (start us, length us, event | category | flops | bytes accessed | tf_op | source)
XLA Modules:
  0.0 50.6 jit_solution(3777955848303991860)
XLA Ops:
  0.6 48.1 %mbconv_attention.1 = (bf16[49,16,128]{2,1,0:T(8,128)(2,1)}, bf16[7,28,512]{2,1,0:T(8,128)(2,1)}) custom-call(bf16[7,28,512]{2,1,0:T(8,128)(2,1)} %x_hbm.1, bf16[7,28,512]{2,1,0:T(8,128)(2,1)} %cot_hbm.1, f32[1,512]{1,0:T(1,128)} %bitcast.11, f32[9,2048]{1,0:T(8,128)} %dw_hbm.1, f32[1,512]{1,0:T(1,128)} %bitcast.12, f32[1,512]{1,0:T(1,128)} %bitcast.13, ...), custom_call_target="tpu_custom_call" | custom-call | tf_op jit(solution)/shard_map/mbconv_attention/pallas_call | solution.py:727
  48.7 1.9 %finish.1 = (bf16[7,28,512]{2,1,0:T(8,128)(2,1)}, bf16[7,28,512]{2,1,0:T(8,128)(2,1)}) custom-call(bf16[49,16,128]{2,1,0:T(8,128)(2,1)} %get-tuple-element.4.chunks_ref, bf16[7,28,512]{2,1,0:T(8,128)(2,1)} %get-tuple-element.5.kept_ref), custom_call_target="tpu_custom_call" | custom-call | tf_op jit(solution)/shard_map/finish/pallas_call | solution.py:742

commit v8 on v7

--- a/solution.py
+++ b/solution.py
@@ -18,6 +18,7 @@
 SW = 32
 NWIN, WPAD = 4, 64
 LEN = 49
+KEYS = 56
 EPSILON = 1e-05
 F32, BF16 = jnp.float32, jnp.bfloat16
 MESH = pl.DeviceIdType.MESH
@@ -467,9 +468,10 @@
             rows = pl.ds(pl.multiple_of(w * WPAD, WPAD), WPAD)
             for g in range(4):
                 q, k, v = parts_of(packed, rows, g)
-                s = dot_nt(k, by_head(q)) * root + bias_t[g]
+                s = dot_nt(k, by_head(q))[0:KEYS] * root + bias_t[g, 0:KEYS, :]
                 e = jnp.exp(s - jnp.max(s, axis=0, keepdims=True))
-                prob[w, g] = e * (1.0 / jnp.sum(e, axis=0, keepdims=True))
+                prob[w, g, 0:KEYS, :] = e * (1.0 / jnp.sum(e, axis=0, keepdims=True))
+                prob[w, g, KEYS:WPAD, :] = jnp.zeros((WPAD - KEYS, 256), F32)
             return carry
 
         lax.fori_loop(0, NWIN, window, 0, unroll=True)
@@ -491,8 +493,10 @@
                 q, k, v = parts_of(packed, rows, g)
                 p = prob[w, g]
                 dam = by_head(da[rows, 128 * g : 128 * (g + 1)])
-                dp = dot_nt(v, dam).astype(BF16).astype(F32)
-                ds = p * (dp - jnp.sum(p * dp, axis=0, keepdims=True))
+                dp = dot_nt(v, dam)[0:KEYS].astype(BF16).astype(F32)
+                inner = p[0:KEYS] * dp
+                ds = p[0:KEYS] * (dp - jnp.sum(inner, axis=0, keepdims=True))
+                ds = jnp.concatenate([ds, jnp.zeros((WPAD - KEYS, 256), F32)], axis=0)
                 ds = ds.astype(BF16)
                 dscore[w, g] = ds
                 dk = dot(ds, by_head(q)) * root

time: 50.8 us -> 50.7 us (level)
  no operation moved by 1% of the time
where the time goes in v8:
time: 50.7 us; the launch traced here: 50.6 us
  Pallas kernels  50 us (99%)
  between operations  0.64 us (1%)
    pallas_call x1, Pallas kernels, local(): pl.pallas_call(kernel, out_shape=(jax.ShapeDtypeStruct((LEN, 16, 128), BF...  48.1 us
    pallas_call x1, Pallas kernels, local(): pl.pallas_call(finish, out_shape=(tokens, tokens), in_specs=[vmem] * 2, o...  1.87 us

profile of v8, /device:TPU:0, one launch (start us, length us, event | category | flops | bytes accessed | tf_op | source)
XLA Modules:
  0.0 50.6 jit_solution(1003680447806006969)
XLA Ops:
  0.6 48.1 %mbconv_attention.1 = (bf16[49,16,128]{2,1,0:T(8,128)(2,1)}, bf16[7,28,512]{2,1,0:T(8,128)(2,1)}) custom-call(bf16[7,28,512]{2,1,0:T(8,128)(2,1)} %x_hbm.1, bf16[7,28,512]{2,1,0:T(8,128)(2,1)} %cot_hbm.1, f32[1,512]{1,0:T(1,128)} %bitcast.11, f32[9,2048]{1,0:T(8,128)} %dw_hbm.1, f32[1,512]{1,0:T(1,128)} %bitcast.12, f32[1,512]{1,0:T(1,128)} %bitcast.13, ...), custom_call_target="tpu_custom_call" | custom-call | tf_op jit(solution)/shard_map/mbconv_attention/pallas_call | solution.py:731
  48.7 1.9 %finish.1 = (bf16[7,28,512]{2,1,0:T(8,128)(2,1)}, bf16[7,28,512]{2,1,0:T(8,128)(2,1)}) custom-call(bf16[49,16,128]{2,1,0:T(8,128)(2,1)} %get-tuple-element.4.chunks_ref, bf16[7,28,512]{2,1,0:T(8,128)(2,1)} %get-tuple-element.5.kept_ref), custom_call_target="tpu_custom_call" | custom-call | tf_op jit(solution)/shard_map/finish/pallas_call | solution.py:746
